TPU v7x, 512 devices: a whole 4x4x16 slice. The times are simulated.
512 devices in a mesh: row: 16 (over y_lo, x, core), col: 32 (over z, y_hi).
Axes of the slice: x: 4, y: 4 (y_hi: 2, y_lo: 2; y = y_hi * 2 + y_lo), z: 16, core: 2. Of those that a mesh axis runs over, the one named last changes fastest.
Arguments:
- fitted_ac: bfloat16 [1600, 16, 4096], P('row', None, 'col'), may hold values from -6 to 6
- fitted_bd: bfloat16 [1600, 8, 4096], P('row', None, 'col'), may hold values from -0.1875 to 0.1875
- amplitudes: bfloat16 [4, 16, 8], P(None, 'row'), may hold values from -0.5 to 0.5
Outputs:
- ladder: float32 [4, 1600, 1600], P(None, 'row', 'col')
All inputs are finite; a program needn't handle non-finite values.
Results may differ from a plain program's by a relative error of at most 0.0029.
Values may be sent and summed in bfloat16 or wider, within the bound.
No kernel may reach another device: no remote copies, remote signals or barrier semaphores. Data moves between devices by JAX's collectives and lax.ppermute only.
A program may use at most 128 MiB of HBM per device.

v0:
```python
import jax
import jax.numpy as jnp
from jax import lax
from jax.sharding import PartitionSpec as P


def on_device(fitted_ac, fitted_bd, amplitudes):
    amp_all = lax.all_gather(amplitudes, "row", axis=1, tiled=True)
    half = jnp.einsum(
        "bdq,pcd->bpcq",
        lax.all_gather(fitted_bd, "row", axis=0, tiled=True),
        amp_all,
        preferred_element_type=jnp.float32,
    ).astype(jnp.bfloat16)
    partial_sum = jnp.einsum("acq,bpcq->pab", fitted_ac, half, preferred_element_type=jnp.float32)
    result = lax.psum_scatter(partial_sum, "col", scatter_dimension=2, tiled=True)
    return result


def solution(mesh):
    return jax.shard_map(
        on_device,
        mesh=mesh,
        in_specs=(P("row", None, "col"), P("row", None, "col"), P(None, "row", None)),
        out_specs=P(None, "row", "col"),
        check_vma=False,
    )
```

profile of v0, /device:TPU:6, one launch (start us, length us, event | category | flops | bytes accessed | tf_op | source)
XLA Modules:
  0.0 422.0 jit_solution(8606441056095577903)
XLA Ops:
  6.5 0.0 all-gather.2.cloned.1.call-start
  6.5 0.7 all-gather.2.cloned.1.call-update
  7.3 0.0 all-reduce.3.cloned.1.call-start
  7.3 19.3 %all_gather.6 = bf16[4,16,8]{2,0,1:T(4,128)(2,1)S(1)} all-gather(bf16[4,1,8]{2,0,1:T(4,128)(2,1)} %param.5), channel_id=1, replica_groups=mesh['row'=16,'col'=32] {'row'}, dimensions={1}, use_global_device_ids=true | all-gather | bytes 1088 | tf_op jit(solution)/shard_map/all_gather | solution.py:8
  26.6 30.0 %all-gather.2.cloned.1.call-done = bf16[1600,8,128]{2,1,0:T(8,128)(2,1)} async-done(((bf16[100,8,128]{2,1,0:T(8,128)(2,1)}), bf16[1600,8,128]{2,1,0:T(8,128)(2,1)}) %all-gather.2.cloned.1.call-update) | async-done | bytes 3276816 | tf_op jit(solution)/shard_map/all_gather | solution.py:11
  56.6 0.0 copy-start
  56.6 14.2 %fusion.3 = bf16[4,16,1600,128]{3,1,2,0:T(8,128)(2,1)} fusion(bf16[1600,8,128]{2,1,0:T(8,128)(2,1)} %all-gather.2.cloned.1.call-done, bf16[4,16,8,1]{2,0,1,3:T(4,128)(2,1)S(1)} %bitcast.18), kind=kOutput, calls=%fused_computation.3 | convolution fusion | flops 209715200 | bytes 29492224 | tf_op jit(solution)/shard_map/bdq,pcd->bpcq/dot_general | solution.py:9
  70.8 0.0 copy-done
  70.8 16.5 %fusion.5 = f32[4,100,1600]{2,1,0:T(8,128)S(1)} fusion(bf16[4,16,1600,128]{3,1,2,0:T(8,128)(2,1)} %fusion.3, bf16[100,16,128]{2,1,0:T(8,128)(2,1)S(1)} %copy-done), kind=kOutput, calls=%fused_computation.5 | convolution fusion | flops 2621440000 | bytes 29184000 | tf_op jit(solution)/shard_map/acq,bpcq->pab/dot_general | solution.py:15
  87.3 3.0 copy.7
  90.3 0.0 all-reduce.3.cloned.1.call-update
  90.4 1.3 dynamic-slice
  92.3 321.3 %all-reduce.3.cloned.1.call-done = f32[4,100,1600]{1,0,2:T(4,128)} async-done(((f32[4,100,1600]{1,0,2:T(4,128)}), f32[4,100,1600]{1,0,2:T(4,128)}) %all-reduce.3.cloned.1.call-update) | async-done | bytes 2560016
  413.6 1.5 constant_dynamic-slice_fusion
Async XLA Ops:
  6.5 50.1 %all-gather.2.cloned.1.call-start = ((), (), s32[]{:S(2)}) async-start(), calls=%async_computation | async-start | bytes 3481600 | tf_op jit(solution)/shard_map/all_gather | solution.py:11
  7.3 406.4 %all-reduce.3.cloned.1.call-start = ((), (), s32[]{:S(2)}) async-start(), calls=%async_computation.1 | async-start | bytes 6553600
  56.6 14.2 %copy-start = (bf16[100,16,128]{2,1,0:T(8,128)(2,1)S(1)}, bf16[100,16,128]{2,1,0:T(8,128)(2,1)}, u32[]{:S(2)}) copy-start(bf16[100,16,128]{2,1,0:T(8,128)(2,1)} %param.3) | copy-start | bytes 1228804
Sparse Core Ops, SparseCore 0:
  9.5 47.0 all-gather.1
  90.5 323.1 all-reduce.2
where the time goes:
time: 422 us
  waiting for transfers between devices  352 us (83%)
  matrix products  30.7 us (7%)
  blocking collectives  19.3 us (5%)
  between operations  14.1 us (3%)
  local copies, waits for them, and re-layouts  5.81 us (1%)
    unnamed x3, waiting for transfers between devices  322 us
    all_gather x1, waiting for transfers between devices, on_device(): lax.all_gather(fitted_bd, 'row', axis=0, tiled=True)  30 us
    all_gather x1, blocking collectives, on_device(): amp_all = lax.all_gather(amplitudes, 'row', axis=1, tiled=True)  19.3 us
    dot_general x1, matrix products, on_device(): jnp.einsum('acq,bpcq->pab', fitted_ac, half, preferred_element_type=jnp.f...  16.5 us
    dot_general x1, matrix products, on_device(): jnp.einsum('bdq,pcd->bpcq', lax.all_gather(fitted_bd, 'row', axis=0, tile...  14.2 us
  transfers between devices with their start and end apart: 2, of which 2 were waited for; matrix products, arithmetic and copies ran while one was open for 0% of the time, Pallas kernels for 0%

commit v1 on v0

v1 whole, which is shorter than its diff:
```python
import jax
import jax.numpy as jnp
from jax import lax
from jax.experimental import pallas as pl
from jax.experimental.pallas import tpu as pltpu
from jax.sharding import Mesh, PartitionSpec as P

ROW = ("yl", "xh", "xl", "core")
COL = ("zq", "zl", "yh")
NT = (((1,), (1,)), ((), ()))
MIB = 1024 * 1024

NA, NB, C, D, NP, Q = 100, 100, 16, 8, 4, 128
ROWS = NA * NP
PAD = 112
PIECE = 160
CHUNKS = (0, 16, 32, 48, 64, 80, 84)


def x_kernel(w_ref, ac_ref, x_ref):
    for a0 in CHUNKS:
        y = jnp.dot(
            w_ref[...], ac_ref[0, a0 * C:(a0 + 16) * C, :], preferred_element_type=jnp.float32
        )
        high = y.astype(jnp.bfloat16)
        low = (y - high.astype(jnp.float32)).astype(jnp.bfloat16)
        for d in range(D):
            rows = slice(a0 * NP, (a0 + 16) * NP)
            x_ref[0, 0, rows, d * Q:(d + 1) * Q] = high[64 * d:64 * (d + 1)]
            x_ref[0, 1, rows, d * Q:(d + 1) * Q] = low[64 * d:64 * (d + 1)]


def make_x(w, ac):
    return pl.pallas_call(
        x_kernel,
        grid=(4,),
        in_specs=[
            pl.BlockSpec((512, 256), lambda k: (0, 0)),
            pl.BlockSpec((1, NA * C, Q), lambda k: (k, 0, 0)),
        ],
        out_specs=pl.BlockSpec((1, 2, ROWS, D * Q), lambda k: (k, 0, 0, 0)),
        out_shape=jax.ShapeDtypeStruct((4, 2, ROWS, D * Q), jnp.bfloat16),
        compiler_params=pltpu.CompilerParams(vmem_limit_bytes=32 * MIB),
        cost_estimate=pl.CostEstimate(flops=2 * 28 * 512 * 256 * 128, bytes_accessed=9 * MIB, transcendentals=0),
        name="make_x",
    )(w, ac)


def product(bd_ref, x_ref):
    left = bd_ref[...].reshape(4 * PAD, 512)
    return lax.dot_general(left, x_ref[0, 0], NT, preferred_element_type=jnp.float32) + lax.dot_general(
        left, x_ref[0, 1], NT, preferred_element_type=jnp.float32
    )


def first_kernel(core_ref, bd_ref, x_ref, acc_ref):
    value = product(bd_ref, x_ref)
    k = pl.program_id(0)

    @pl.when(k == 0)
    def _():
        acc_ref[...] = value

    @pl.when(k > 0)
    def _():
        acc_ref[...] += value


def second_kernel(core_ref, bd_ref, x_ref, before_ref, out_ref, acc_ref, piece_ref):
    value = product(bd_ref, x_ref)
    k = pl.program_id(0)

    @pl.when(k == 0)
    def _():
        acc_ref[...] = before_ref[...] + value

    @pl.when(k > 0)
    def _():
        acc_ref[...] += value

    @pl.when(k == 3)
    def _():
        for t in range(4):
            for yh in range(2):
                at = t * PAD + 50 * yh
                for j in range(3):
                    piece_ref[50 * j:50 * j + 50, :] = acc_ref[at:at + 50, 128 * j:128 * (j + 1)]
                rest = [acc_ref[at + 10 * g:at + 10 * g + 10, 384:400] for g in range(5)]
                piece_ref[150:160, :] = jnp.concatenate(rest + [jnp.zeros((10, 48), jnp.float32)], axis=1)
                out_ref[2 * t + yh] = piece_ref[...].astype(jnp.bfloat16)


def multiply(core, bd, x, before=None):
    bd_spec = pl.BlockSpec((4, None, PAD, 512), lambda k, core_ref: (0, k // 2, 0, k % 2))
    x_spec = pl.BlockSpec((1, 2, ROWS, 512), lambda k, core_ref: (2 * (k // 2) + core_ref[0], 0, 0, k % 2))
    acc_spec = pl.BlockSpec((4 * PAD, ROWS), lambda k, core_ref: (0, 0))
    acc_shape = jax.ShapeDtypeStruct((4 * PAD, ROWS), jnp.float32)
    cost = pl.CostEstimate(flops=2 * 2 * 400 * 400 * 2048, bytes_accessed=6 * MIB, transcendentals=0)
    params = pltpu.CompilerParams(vmem_limit_bytes=32 * MIB)
    if before is None:
        return pl.pallas_call(
            first_kernel,
            grid_spec=pltpu.PrefetchScalarGridSpec(
                num_scalar_prefetch=1, grid=(4,), in_specs=[bd_spec, x_spec], out_specs=acc_spec
            ),
            out_shape=acc_shape,
            compiler_params=params,
            cost_estimate=cost,
            name="first_half",
        )(core, bd, x)
    return pl.pallas_call(
        second_kernel,
        grid_spec=pltpu.PrefetchScalarGridSpec(
            num_scalar_prefetch=1,
            grid=(4,),
            in_specs=[bd_spec, x_spec, acc_spec],
            out_specs=pl.BlockSpec((8, PIECE, 128), lambda k, core_ref: (0, 0, 0)),
            scratch_shapes=[pltpu.VMEM((4 * PAD, ROWS), jnp.float32), pltpu.VMEM((PIECE, 128), jnp.float32)],
        ),
        out_shape=jax.ShapeDtypeStruct((8, PIECE, 128), jnp.bfloat16),
        compiler_params=params,
        cost_estimate=cost,
        name="second_half",
    )(core, bd, x, before)


def last_kernel(parts_ref, out_ref, sum_ref, turned_ref):
    sum_ref[...] = jnp.sum(parts_ref[...].astype(jnp.float32), axis=0)
    for j in range(3):
        turned_ref[128 * j:128 * (j + 1), :] = sum_ref[50 * j:50 * j + 50, :].T
    rest = sum_ref[150:160, :].T
    for g in range(5):
        turned_ref[384:400, 10 * g:10 * g + 10] = rest[16 * g:16 * (g + 1), :]
    for p in range(NP):
        out_ref[p] = turned_ref[pl.ds(p, NA, stride=NP), :]


def finish(parts):
    return pl.pallas_call(
        last_kernel,
        in_specs=[pl.BlockSpec(memory_space=pltpu.VMEM)],
        out_specs=pl.BlockSpec(memory_space=pltpu.VMEM),
        out_shape=jax.ShapeDtypeStruct((NP, NA, 50), jnp.float32),
        scratch_shapes=[pltpu.VMEM((PIECE, 128), jnp.float32), pltpu.VMEM((ROWS, 50), jnp.float32)],
        name="finish",
    )(parts)


def on_device(fitted_ac, fitted_bd, amplitudes):
    core = lax.axis_index("core").astype(jnp.int32)
    turn = [(4 * u + v, 4 * v + u) for u in range(4) for v in range(4)]
    mine = lax.ppermute(fitted_bd.reshape(NB, D * Q), ("xl", "core", "zl"), turn)
    ac_all = lax.all_to_all(
        jnp.broadcast_to(fitted_ac[None], (4,) + fitted_ac.shape), "zl", 0, 0, tiled=True
    ).reshape(4, NA * C, Q)
    bd_own = lax.all_to_all(
        jnp.broadcast_to(mine[None], (8,) + mine.shape), ("yl", "xh", "xl"), 0, 0, tiled=True
    )
    amp = lax.all_gather(amplitudes, ROW, axis=1, tiled=True)
    w = (
        jnp.transpose(amp, (2, 0, 1))[:, None, :, None, :] * jnp.eye(16, dtype=amp.dtype)[None, :, None, :, None]
    ).reshape(512, 256)
    x = make_x(w, ac_all)
    bd_other = lax.ppermute(bd_own, "core", [(0, 1), (1, 0)])
    acc = multiply(core[None], bd_own.reshape(4, 2, NB, D * Q), x)
    pieces = multiply((1 - core)[None], bd_other.reshape(4, 2, NB, D * Q), x, acc)
    return finish(lax.all_to_all(pieces, ("zq", "yh"), 0, 0, tiled=True))


def solution(mesh):
    fine = Mesh(mesh.devices.reshape(2, 2, 2, 2, 4, 4, 2), ROW + COL)
    return jax.shard_map(
        on_device,
        mesh=fine,
        in_specs=(P(ROW, None, COL), P(ROW, None, COL), P(None, ROW, None)),
        out_specs=P(None, ROW, COL),
        check_vma=False,
    )
```

time: 422 us -> 144 us (0.34)
  the two profiles are of different devices: /device:TPU:6 before, /device:TPU:1 now
where the time goes in v1:
time: 144 us
  blocking collectives  83.5 us (58%)
  starting transfers between devices  18.5 us (13%)
  waiting for transfers between devices  14.3 us (10%)
  Pallas kernels  13.3 us (9%)
  local copies, waits for them, and re-layouts  12.4 us (9%)
  other arithmetic  1.57 us (1%)
    all_to_all x1, blocking collectives, on_device(): return finish(lax.all_to_all(pieces, ('zq', 'yh'), 0, 0, tiled=True))  38.7 us
    all_to_all x1, blocking collectives, on_device(): lax.all_to_all(jnp.broadcast_to(mine[None], (8,) + mine.shape), ('yl', 'x...  27.1 us
    all_gather x1, blocking collectives, on_device(): amp = lax.all_gather(amplitudes, ROW, axis=1, tiled=True)  17.7 us
    all_to_all x1, starting transfers between devices, on_device(): lax.all_to_all(jnp.broadcast_to(fitted_ac[None], (4,) + fitted_ac.shape),...  11.6 us
    all_to_all x1, waiting for transfers between devices, on_device(): lax.all_to_all(jnp.broadcast_to(fitted_ac[None], (4,) + fitted_ac.shape),...  10.6 us
    ppermute x1, starting transfers between devices, on_device(): lax.ppermute(fitted_bd.reshape(NB, D * Q), ('xl', 'core', 'zl'), turn)  4.94 us
    pallas_call x1, Pallas kernels, make_x(): pl.pallas_call(x_kernel, grid=(4,), in_specs=[pl.BlockSpec((512, 256), la...  4.23 us
    mul x1, local copies, waits for them, and re-layouts, on_device(): jnp.transpose(amp, (2, 0, 1))[:, None, :, None, :]  3.86 us
  transfers between devices with their start and end apart: 3, of which 2 were waited for; matrix products, arithmetic and copies ran while one was open for 6% of the time, Pallas kernels for 0%

profile of v1, /device:TPU:1, one launch (start us, length us, event | category | flops | bytes accessed | tf_op | source)
XLA Modules:
  0.0 143.5 jit_solution(1020065517614434094)
XLA Ops:
  0.0 0.9 pad
  1.0 4.9 %collective-permute-start = (bf16[100,1024]{1,0:T(8,128)(2,1)S(1)}, bf16[100,1024]{1,0:T(8,128)(2,1)S(1)}, u32[]{:S(2)}, u32[]{:S(2)}) collective-permute-start(bf16[100,1024]{1,0:T(8,128)(2,1)S(1)} %bitcast.14), channel_id=1, source_target_pairs={{0,0},{2,32},{4,64},{6,96},{32,2},{34,34},{36,66},{38,98},{64,4},{... | collective-permute-start | bytes 614408 | tf_op jit(solution)/shard_map/ppermute | solution.py:152
  5.9 3.7 %collective-permute-done = bf16[100,1024]{1,0:T(8,128)(2,1)S(1)} collective-permute-done((bf16[100,1024]{1,0:T(8,128)(2,1)S(1)}, bf16[100,1024]{1,0:T(8,128)(2,1)S(1)}, u32[]{:S(2)}, u32[]{:S(2)}) %collective-permute-start) | collective-permute-done | bytes 204832 | tf_op jit(solution)/shard_map/ppermute | solution.py:152
  9.6 0.2 broadcast_in_dim.9
  9.8 0.0 copy-start.1
  9.8 27.1 %all_to_all.15 = bf16[8,100,1024]{2,1,0:T(8,128)(2,1)S(1)} all-to-all(bf16[8,100,1024]{2,1,0:T(8,128)(2,1)S(1)} %broadcast_in_dim.9), channel_id=1, replica_groups=mesh['yl'=2,'xh'=2,'xl'=2,'core'=2,'zq'=4,'zl'=4,'yh'=2] {'yl','xh','xl'}, dimensions={0} | all-to-all | bytes 3276800 | tf_op jit(solution)/shard_map/all_to_all | solution.py:156
  36.9 0.0 copy-done.1
  36.9 1.4 broadcast_in_dim.10
  38.3 11.6 %all-to-all-start.1 = ((bf16[4,100,16,128]{3,2,1,0:T(8,128)(2,1)}), bf16[4,100,16,128]{3,2,1,0:T(8,128)(2,1)}, u32[]{:S(2)}, u32[]{:S(2)}) async-start(bf16[4,100,16,128]{3,2,1,0:T(8,128)(2,1)} %broadcast_in_dim.10), calls=%async_computation.1 | async-start | bytes 3276800 | tf_op jit(solution)/shard_map/all_to_all | solution.py:153
  49.9 0.0 copy-start.2
  49.9 0.9 copy.10
  50.8 1.9 %collective-permute-start.1 = (bf16[8,100,1024]{2,0,1:T(8,128)(2,1)S(1)}, bf16[8,100,1024]{2,0,1:T(8,128)(2,1)}, u32[]{:S(2)}, u32[]{:S(2)}) collective-permute-start(bf16[8,100,1024]{2,0,1:T(8,128)(2,1)S(1)} %copy.10), channel_id=1, source_target_pairs={{0,32},{32,0},{1,33},{33,1},{2,34},{34,2},{3,35},{35,3},{4,36},{36... | collective-permute-start | bytes 4915208 | tf_op jit(solution)/shard_map/ppermute | solution.py:164
  52.7 0.0 copy-done.2
  52.7 17.7 %all_gather.3 = bf16[4,16,8]{2,0,1:T(4,128)(2,1)S(1)} all-gather(bf16[4,1,8]{2,0,1:T(4,128)(2,1)S(1)} %copy-done.2), channel_id=1, replica_groups=mesh['yl'=2,'xh'=2,'xl'=2,'core'=2,'zq'=4,'zl'=4,'yh'=2] {'yl','xh','xl'..., dimensions={1}, use_global_device_ids=true | all-gather | bytes 1088 | tf_op jit(solution)/shard_map/all_gather | solution.py:159
  70.4 0.1 copy.12
  70.5 1.6 %broadcast_multiply_fusion = bf16[8,16,4,16,16]{4,3,2,1,0:T(8,128)(2,1)} fusion(bf16[16,16]{1,0:T(8,128)(2,1)S(1)} %fusion, bf16[8,4,16]{2,1,0:T(4,128)(2,1)S(1)} %copy.12), kind=kLoop, calls=%fused_computation | loop fusion | flops 131072 | bytes 263680 | tf_op jit(solution)/shard_map/mul | solution.py:161
  72.1 3.9 %mul.20.w_ref = bf16[512,256]{1,0:T(8,128)(2,1)} reshape(bf16[8,16,4,16,16]{4,3,2,1,0:T(8,128)(2,1)} %broadcast_multiply_fusion) | data formatting | bytes 524288 | tf_op jit(solution)/shard_map/mul | solution.py:161
  76.0 0.0 collective-permute-done.1
  76.0 2.3 %copy.11 = bf16[8,100,1024]{2,1,0:T(8,128)(2,1)S(1)} copy(bf16[8,100,1024]{2,0,1:T(8,128)(2,1)} %collective-permute-done.1) | data formatting | bytes 3276800 | tf_op jit(solution)/shard_map/ppermute | solution.py:164
  78.3 10.6 %all-to-all-done.1 = bf16[4,100,16,128]{3,2,1,0:T(8,128)(2,1)} async-done(((bf16[4,100,16,128]{3,2,1,0:T(8,128)(2,1)}), bf16[4,100,16,128]{3,2,1,0:T(8,128)(2,1)}, u32[]{:S(2)}, u32[]{:S(2)}) %all-to-all-start.1) | async-done | bytes 1638432 | tf_op jit(solution)/shard_map/all_to_all | solution.py:153
  88.9 0.0 copy-start
  88.9 0.9 copy-done
  89.8 4.2 %make_x.1.x_ref = bf16[4,2,400,1024]{3,2,1,0:T(8,128)(2,1)S(1)} custom-call(bf16[512,256]{1,0:T(8,128)(2,1)S(1)} %copy-done, bf16[4,1600,128]{2,1,0:T(8,128)(2,1)} %bitcast.3.ac_ref), custom_call_target="tpu_custom_call" | custom-call | flops 939524096 | bytes 9437184 | tf_op jit(solution)/shard_map/make_x/pallas_call | solution.py:34
  94.1 3.5 %first_half.1.before_ref = f32[448,400]{1,0:T(8,128)S(1)} custom-call(s32[1]{0:T(128)} %bitcast.4.core_ref, bf16[4,2,100,1024]{3,2,1,0:T(8,128)(2,1)S(1)} %bitcast.11, bf16[4,2,400,1024]{3,2,1,0:T(8,128)(2,1)S(1)} %make_x.1.x_ref), custom_call_target="tpu_custom_call" | custom-call | flops 1310720000 | bytes 6291456 | tf_op jit(solution)/shard_map/first_half/pallas_call | solution.py:101
  97.5 3.7 %second_half.1 = bf16[8,160,128]{2,1,0:T(8,128)(2,1)S(1)} custom-call(s32[1]{0:T(128)} %bitcast.core_ref, bf16[4,2,100,1024]{3,2,1,0:T(8,128)(2,1)S(1)} %bitcast.12, bf16[4,2,400,1024]{3,2,1,0:T(8,128)(2,1)S(1)} %make_x.1.x_ref, f32[448,400]{1,0:T(8,128)S(1)} %first_half.1.before_ref), custom_call_target="tpu_custom_call" | custom-call | flops 1310720000 | bytes 6291456 | tf_op jit(solution)/shard_map/second_half/pallas_call | solution.py:111
  101.3 38.7 %all_to_all.16.parts_ref = bf16[8,160,128]{2,1,0:T(8,128)(2,1)} all-to-all(bf16[8,160,128]{2,1,0:T(8,128)(2,1)S(1)} %second_half.1), channel_id=1, replica_groups=mesh['yl'=2,'xh'=2,'xl'=2,'core'=2,'zq'=4,'zl'=4,'yh'=2] {'zq','yh'}, dimensions={0} | all-to-all | bytes 655360 | tf_op jit(solution)/shard_map/all_to_all | solution.py:167
  139.9 1.9 %finish.1 = f32[4,100,50]{2,1,0:T(8,128)} custom-call(bf16[8,160,128]{2,1,0:T(8,128)(2,1)} %all_to_all.16.parts_ref), custom_call_target="tpu_custom_call" | custom-call | tf_op jit(solution)/shard_map/finish/pallas_call | solution.py:139
  141.8 1.7 %copy.13 = f32[4,100,50]{1,0,2:T(4,128)} copy(f32[4,100,50]{2,1,0:T(8,128)} %finish.1) | data formatting | bytes 160000 | tf_op jit(solution)/shard_map/finish/pallas_call | solution.py:139
  (2 shorter events, 0.0 us)
Async XLA Ops:
  1.0 8.6 %collective-permute-start = (bf16[100,1024]{1,0:T(8,128)(2,1)S(1)}, bf16[100,1024]{1,0:T(8,128)(2,1)S(1)}, u32[]{:S(2)}, u32[]{:S(2)}) collective-permute-start(bf16[100,1024]{1,0:T(8,128)(2,1)S(1)} %bitcast.14), channel_id=1, source_target_pairs={{0,0},{2,32},{4,64},{6,96},{32,2},{34,34},{36,66},{38,98},{64,4},{... | collective-permute-start | bytes 614408 | tf_op jit(solution)/shard_map/ppermute | solution.py:152
  9.8 27.1 %copy-start.1 = (bf16[100,16,128]{2,1,0:T(8,128)(2,1)S(1)}, bf16[100,16,128]{2,1,0:T(8,128)(2,1)}, u32[]{:S(2)}) copy-start(bf16[100,16,128]{2,1,0:T(8,128)(2,1)} %param.3) | copy-start | bytes 1228804
  38.3 50.6 %all-to-all-start.1 = ((bf16[4,100,16,128]{3,2,1,0:T(8,128)(2,1)}), bf16[4,100,16,128]{3,2,1,0:T(8,128)(2,1)}, u32[]{:S(2)}, u32[]{:S(2)}) async-start(bf16[4,100,16,128]{3,2,1,0:T(8,128)(2,1)} %broadcast_in_dim.10), calls=%async_computation.1 | async-start | bytes 3276800 | tf_op jit(solution)/shard_map/all_to_all | solution.py:153
  49.9 2.8 %copy-start.2 = (bf16[4,1,8]{2,0,1:T(4,128)(2,1)S(1)}, bf16[4,1,8]{2,0,1:T(4,128)(2,1)}, u32[]{:S(2)}) copy-start(bf16[4,1,8]{2,0,1:T(4,128)(2,1)} %param.5) | copy-start | bytes 196
  50.8 25.2 %collective-permute-start.1 = (bf16[8,100,1024]{2,0,1:T(8,128)(2,1)S(1)}, bf16[8,100,1024]{2,0,1:T(8,128)(2,1)}, u32[]{:S(2)}, u32[]{:S(2)}) collective-permute-start(bf16[8,100,1024]{2,0,1:T(8,128)(2,1)S(1)} %copy.10), channel_id=1, source_target_pairs={{0,32},{32,0},{1,33},{33,1},{2,34},{34,2},{3,35},{35,3},{4,36},{36... | collective-permute-start | bytes 4915208 | tf_op jit(solution)/shard_map/ppermute | solution.py:164
  88.9 1.0 copy-start

commit v2 on v0

v2 whole, which is shorter than its diff:
```python
import jax
import jax.numpy as jnp
from jax import lax
from jax.experimental import pallas as pl
from jax.experimental.pallas import tpu as pltpu
from jax.sharding import Mesh, PartitionSpec as P

ROW = ("yl", "x", "core")
COL = ("zh", "zp", "yh")
NT = (((1,), (1,)), ((), ()))
MIB = 1024 * 1024

NA, NB, C, D, NP, Q = 100, 100, 16, 8, 4, 128
ROWS = NA * NP
HALF = 50
UNIT = 56
PAD = 64
PIECE = 160


def spread(amp, wide):
    tall, across = D * NP * wide, wide * C
    row = lax.broadcasted_iota(jnp.int32, (tall, D * NP), 0)
    col = lax.broadcasted_iota(jnp.int32, (tall, D * NP), 1)
    pick_row = jnp.where(row // wide == col, 1.0, 0.0).astype(jnp.bfloat16)
    row = lax.broadcasted_iota(jnp.int32, (C, across), 0)
    col = lax.broadcasted_iota(jnp.int32, (C, across), 1)
    pick_col = jnp.where(col % C == row, 1.0, 0.0).astype(jnp.bfloat16)
    wider = jnp.dot(pick_row, amp.T, preferred_element_type=jnp.float32).astype(jnp.bfloat16)
    full = jnp.dot(wider, pick_col, preferred_element_type=jnp.float32)
    row = lax.broadcasted_iota(jnp.int32, (tall, across), 0)
    col = lax.broadcasted_iota(jnp.int32, (tall, across), 1)
    return jnp.where(row % wide == col // C, full, 0.0).astype(jnp.bfloat16)


def product_kernel(m_ref, amp_ref, ac00_ref, ac01_ref, ac10_ref, ac11_ref, bd_ref, out_ref, ac_ref, x_ref, left_ref, acc_ref):
    for m, pair in enumerate(((ac00_ref, ac10_ref), (ac01_ref, ac11_ref))):

        @pl.when(m_ref[0] == m)
        def _():
            for dy in range(2):
                ac_ref[:, dy * Q:(dy + 1) * Q] = pair[dy][...]

    for dy in range(2):
        for t in range(8):
            left_ref[t, 0:UNIT, dy * D * Q:(dy + 1) * D * Q] = bd_ref[t, dy]
    w16, w4 = spread(amp_ref[...], 16), spread(amp_ref[...], 4)
    for k in range(7):
        w, n = (w16, 16) if k < 6 else (w4, 4)
        y = jnp.dot(w, ac_ref[k * 256:k * 256 + n * C, :], preferred_element_type=jnp.float32)
        high = y.astype(jnp.bfloat16)
        low = (y - high.astype(jnp.float32)).astype(jnp.bfloat16)
        tall = NP * n
        for dy in range(2):
            for d in range(D):
                rows, columns = slice(64 * k, 64 * k + tall), slice((dy * D + d) * Q, (dy * D + d + 1) * Q)
                here = slice(tall * d, tall * (d + 1)), slice(Q * dy, Q * (dy + 1))
                x_ref[0, rows, columns] = high[here]
                x_ref[1, rows, columns] = low[here]
    left = left_ref[...].reshape(8 * PAD, 2 * D * Q)
    acc_ref[...] = lax.dot_general(left, x_ref[0], NT, preferred_element_type=jnp.float32) + lax.dot_general(
        left, x_ref[1], NT, preferred_element_type=jnp.float32
    )
    for t in range(8):
        at = t * PAD
        for j in range(3):
            out_ref[t, 50 * j:50 * j + 50, :] = acc_ref[at:at + 50, 128 * j:128 * (j + 1)]
        rest = [acc_ref[at + 10 * g:at + 10 * g + 10, 384:400] for g in range(5)]
        out_ref[t, 150:160, :] = jnp.concatenate(rest + [jnp.zeros((10, 48), jnp.float32)], axis=1)


def multiply(m, amp, blocks, bd):
    return pl.pallas_call(
        product_kernel,
        in_specs=[pl.BlockSpec(memory_space=pltpu.SMEM)] + [pl.BlockSpec(memory_space=pltpu.VMEM)] * 6,
        out_specs=pl.BlockSpec(memory_space=pltpu.VMEM),
        scratch_shapes=[
            pltpu.VMEM((NA * C, 2 * Q), jnp.bfloat16),
            pltpu.VMEM((2, ROWS, 2 * D * Q), jnp.bfloat16),
            pltpu.VMEM((8, PAD, 2 * D * Q), jnp.bfloat16),
            pltpu.VMEM((8 * PAD, ROWS), jnp.float32),
        ],
        out_shape=jax.ShapeDtypeStruct((8, PIECE, 128), jnp.float32),
        compiler_params=pltpu.CompilerParams(vmem_limit_bytes=32 * MIB),
        cost_estimate=pl.CostEstimate(flops=2 * 2 * 400 * 400 * 2048, bytes_accessed=6 * MIB, transcendentals=0),
        name="multiply",
    )(m, amp, *blocks, bd)


def last_kernel(parts_ref, out_ref, sum_ref):
    sum_ref[...] = jnp.sum(parts_ref[...].astype(jnp.float32), axis=0)
    rest = jnp.concatenate([sum_ref[150:160, 16 * g:16 * (g + 1)] for g in range(5)], axis=0)
    for p in range(NP):
        pieces = [sum_ref[50 * (k // 2):50 * (k // 2) + 50, 64 * (k % 2) + 16 * p:64 * (k % 2) + 16 * p + 16] for k in range(6)]
        out_ref[:, p, :] = jnp.concatenate(pieces + [rest[:, 4 * p:4 * p + 4]], axis=1)


def finish(parts):
    return pl.pallas_call(
        last_kernel,
        in_specs=[pl.BlockSpec(memory_space=pltpu.VMEM)],
        out_specs=pl.BlockSpec(memory_space=pltpu.VMEM),
        out_shape=jax.ShapeDtypeStruct((50, NP, NA), jnp.float32),
        scratch_shapes=[pltpu.VMEM((PIECE, 128), jnp.float32)],
        name="finish",
    )(parts)


def on_device(fitted_ac, fitted_bd, amplitudes):
    core, zp, yh = (lax.axis_index(name) for name in ("core", "zp", "yh"))
    group = ("core", "zp", "yh")

    def sent(array, place):
        ways = []
        for e in range(2):
            for z in range(2):
                for y in range(2):
                    to = place(e, z, y)
                    ways.append((4 * e + 2 * z + y, 4 * to[0] + 2 * to[1] + to[2]))
        return lax.ppermute(array, group, ways)

    ac = fitted_ac.reshape(NA * C, Q)
    across = sent(ac, lambda e, z, y: (e, z, y ^ 1))
    blocks = [sent(array, lambda e, z, y: (z, e ^ m, y)) for array in (ac, across) for m in range(2)]

    halves = fitted_bd.reshape(2, HALF, D * Q)
    units = []
    for dy in range(2):
        half = lax.dynamic_index_in_dim(halves, yh ^ dy, 0, keepdims=False)
        half = jnp.pad(half, ((0, UNIT - HALF), (0, 0)))
        units.append(sent(half, lambda e, z, y: (z, e, y ^ dy)))
    flat = jnp.transpose(amplitudes, (1, 2, 0)).reshape(D * NP)
    peer = lax.ppermute(flat, "core", [(0, 1), (1, 0)])
    two = jnp.where(core == 0, jnp.concatenate([flat, peer]), jnp.concatenate([peer, flat]))
    both = jnp.stack(units) + jnp.pad(two[None, None], ((0, 1), (HALF, UNIT - HALF - 1), (0, D * Q - 2 * D * NP)))
    bd = lax.all_to_all(jnp.broadcast_to(both[None], (8,) + both.shape), ("yl", "x"), 0, 0, tiled=True)
    amp = bd[:, 0, HALF, :2 * D * NP].reshape(C, D * NP)

    m = (zp ^ core).astype(jnp.int32)[None]
    for_other = multiply(m ^ 1, amp, blocks, bd)
    for_self = multiply(m, amp, blocks, bd)
    pieces = (for_self + lax.ppermute(for_other, "core", [(0, 1), (1, 0)])).astype(jnp.bfloat16)
    summed = finish(lax.all_to_all(pieces, "zh", 0, 0, tiled=True))
    return jnp.transpose(summed, (1, 2, 0))


def solution(mesh):
    fine = Mesh(mesh.devices.reshape(2, 4, 2, 8, 2, 2), ROW + COL)
    return jax.shard_map(
        on_device,
        mesh=fine,
        in_specs=(P(ROW, None, COL), P(ROW, None, COL), P(None, ROW, None)),
        out_specs=P(None, ROW, COL),
        check_vma=False,
    )
```

time: 422 us -> 116 us (0.27)
  the two profiles are of different devices: /device:TPU:6 before, /device:TPU:2 now
where the time goes in v2:
time: 116 us; the launch traced here: 115 us
  blocking collectives  39.3 us (34%)
  starting transfers between devices  32.4 us (28%)
  waiting for transfers between devices  30.6 us (26%)
  Pallas kernels  8.82 us (8%)
  local copies, waits for them, and re-layouts  3.61 us (3%)
    all_to_all x1, blocking collectives, on_device(): summed = finish(lax.all_to_all(pieces, 'zh', 0, 0, tiled=True))  39.3 us
    ppermute x7, waiting for transfers between devices, sent(): return lax.ppermute(array, group, ways)  29.9 us
    ppermute x7, starting transfers between devices, sent(): return lax.ppermute(array, group, ways)  19.7 us
    pallas_call x2, Pallas kernels, multiply(): pl.pallas_call(product_kernel, in_specs=[pl.BlockSpec(memory_space=pltpu....  6.91 us
    all_to_all x1, starting transfers between devices, on_device(): lax.all_to_all(jnp.broadcast_to(both[None], (8,) + both.shape), ('yl', 'x...  5.42 us
    ppermute x1, starting transfers between devices, on_device(): peer = lax.ppermute(flat, 'core', [(0, 1), (1, 0)])  4.62 us
    ppermute x1, starting transfers between devices, on_device(): lax.ppermute(for_other, 'core', [(0, 1), (1, 0)])  2.67 us
  transfers between devices with their start and end apart: 10, of which 3 were waited for; matrix products, arithmetic and copies ran while one was open for 1% of the time, Pallas kernels for 3%

profile of v2, /device:TPU:2, one launch (start us, length us, event | category | flops | bytes accessed | tf_op | source)
XLA Modules:
  0.0 115.1 jit_solution(12466169583643605081)
XLA Ops:
  0.0 1.0 reshape.67
  1.1 5.1 %collective-permute-start.1 = (bf16[56,1024]{1,0:T(8,128)(2,1)S(1)}, bf16[56,1024]{1,0:T(8,128)(2,1)S(1)}, u32[]{:S(2)}, u32[]{:S(2)}) collective-permute-start(bf16[56,1024]{1,0:T(8,128)(2,1)S(1)} %pad.12), channel_id=1, source_target_pairs={{0,1},{1,0},{2,33},{3,32},{32,3},{33,2},{34,35},{35,34},{4,5},{5,4... | collective-permute-start | bytes 344072 | tf_op jit(solution)/shard_map/ppermute | solution.py:120
  6.2 0.7 collective-permute-start
  6.9 0.8 copy.6
  7.7 0.1 reshape.68
  7.8 4.6 %collective-permute-start.2 = (bf16[32]{0:T(256)(128)(2,1)S(1)}, bf16[32]{0:T(256)(128)(2,1)S(1)}, u32[]{:S(2)}, u32[]{:S(2)}) collective-permute-start(bf16[32]{0:T(256)(128)(2,1)S(1)} %reshape.68), channel_id=1, source_target_pairs={{0,32},{32,0},{1,33},{33,1},{2,34},{34,2},{3,35},{35,3},{4,36},{36... | collective-permute-start | bytes 200 | tf_op jit(solution)/shard_map/ppermute | solution.py:133
  12.4 0.1 concatenate.24
  12.5 0.7 collective-permute-done.2
  13.2 0.1 broadcast_select_fusion
  13.3 0.0 collective-permute-done.1
  13.3 0.0 collective-permute-done
  13.3 1.5 %broadcast_in_dim.5 = bf16[8,2,56,1024]{3,2,1,0:T(8,128)(2,1)} broadcast(bf16[2,56,1024]{2,1,0:T(8,128)(2,1)S(1)} %maximum_add_fusion), dimensions={1,2,3} | broadcast | bytes 2064384 | tf_op jit(solution)/shard_map/broadcast_in_dim | solution.py:136
  14.8 5.4 %all-to-all-start = ((bf16[8,2,56,1024]{3,2,1,0:T(8,128)(2,1)}), bf16[8,2,56,1024]{3,2,1,0:T(8,128)(2,1)S(1)}, u32[]{:S(2)}, u32[]{:S(2)}) async-start(bf16[8,2,56,1024]{3,2,1,0:T(8,128)(2,1)} %broadcast_in_dim.5), calls=%async_computation | async-start | bytes 3670016 | tf_op jit(solution)/shard_map/all_to_all | solution.py:136
  20.2 3.8 %collective-permute-start.5 = (bf16[1600,128]{1,0:T(8,128)(2,1)}, bf16[1600,128]{1,0:T(8,128)(2,1)}, u32[]{:S(2)}, u32[]{:S(2)}) collective-permute-start(bf16[1600,128]{1,0:T(8,128)(2,1)} %bitcast.7), channel_id=1, source_target_pairs={{0,1},{1,0},{2,3},{3,2},{32,33},{33,32},{34,35},{35,34},{4,5},{5,4... | collective-permute-start | bytes 1228808 | tf_op jit(solution)/shard_map/ppermute | solution.py:120
  24.0 1.7 %collective-permute-start.3 = (bf16[1600,128]{1,0:T(8,128)(2,1)}, bf16[1600,128]{1,0:T(8,128)(2,1)S(1)}, u32[]{:S(2)}, u32[]{:S(2)}) collective-permute-start(bf16[1600,128]{1,0:T(8,128)(2,1)} %bitcast.7), channel_id=1, source_target_pairs={{0,0},{1,1},{2,32},{3,33},{32,2},{33,3},{34,34},{35,35},{4,4},{5,5... | collective-permute-start | bytes 1228808 | tf_op jit(solution)/shard_map/ppermute | solution.py:120
  25.7 3.6 %collective-permute-start.4 = (bf16[1600,128]{1,0:T(8,128)(2,1)}, bf16[1600,128]{1,0:T(8,128)(2,1)S(1)}, u32[]{:S(2)}, u32[]{:S(2)}) collective-permute-start(bf16[1600,128]{1,0:T(8,128)(2,1)} %bitcast.7), channel_id=1, source_target_pairs={{0,2},{1,3},{2,34},{3,35},{32,0},{33,1},{34,32},{35,33},{4,6},{5,7... | collective-permute-start | bytes 1228808 | tf_op jit(solution)/shard_map/ppermute | solution.py:120
  29.2 22.4 %collective-permute-done.5 = bf16[1600,128]{1,0:T(8,128)(2,1)} collective-permute-done((bf16[1600,128]{1,0:T(8,128)(2,1)}, bf16[1600,128]{1,0:T(8,128)(2,1)}, u32[]{:S(2)}, u32[]{:S(2)}) %collective-permute-start.5) | collective-permute-done | bytes 409632 | tf_op jit(solution)/shard_map/ppermute | solution.py:120
  51.6 1.6 %collective-permute-start.6 = (bf16[1600,128]{1,0:T(8,128)(2,1)}, bf16[1600,128]{1,0:T(8,128)(2,1)S(1)}, u32[]{:S(2)}, u32[]{:S(2)}) collective-permute-start(bf16[1600,128]{1,0:T(8,128)(2,1)} %collective-permute-done.5), channel_id=1, source_target_pairs={{0,0},{1,1},{2,32},{3,33},{32,2},{33,3},{34,34},{35,35},{4,4},{5,5... | collective-permute-start | bytes 1228808 | tf_op jit(solution)/shard_map/ppermute | solution.py:120
  53.3 3.3 %collective-permute-start.7 = (bf16[1600,128]{1,0:T(8,128)(2,1)}, bf16[1600,128]{1,0:T(8,128)(2,1)S(1)}, u32[]{:S(2)}, u32[]{:S(2)}) collective-permute-start(bf16[1600,128]{1,0:T(8,128)(2,1)} %collective-permute-done.5), channel_id=1, source_target_pairs={{0,2},{1,3},{2,34},{3,35},{32,0},{33,1},{34,32},{35,33},{4,6},{5,7... | collective-permute-start | bytes 1228808 | tf_op jit(solution)/shard_map/ppermute | solution.py:120
  56.6 0.0 all-to-all-done.bd_ref
  56.6 0.1 reshape_squeeze.3.amp_ref
  56.7 0.0 collective-permute-done.3.ac00_ref
  56.7 0.0 collective-permute-done.4.ac01_ref
  56.7 0.0 collective-permute-done.6.ac10_ref
  56.7 7.5 %collective-permute-done.7.ac11_ref = bf16[1600,128]{1,0:T(8,128)(2,1)S(1)} collective-permute-done((bf16[1600,128]{1,0:T(8,128)(2,1)}, bf16[1600,128]{1,0:T(8,128)(2,1)S(1)}, u32[]{:S(2)}, u32[]{:S(2)}) %collective-permute-start.7) | collective-permute-done | bytes 409632 | tf_op jit(solution)/shard_map/ppermute | solution.py:120
  64.2 3.4 %multiply.3 = f32[8,160,128]{2,1,0:T(8,128)S(1)} custom-call(s32[1]{0:T(128)S(6)} %xor.11.m_ref, bf16[16,32]{1,0:T(8,128)(2,1)S(1)} %reshape_squeeze.3.amp_ref, bf16[1600,128]{1,0:T(8,128)(2,1)S(1)} %collective-permute-done.3.ac00_ref, bf16[1600,128]{1,0:T(8,128)(2,1)S(1)} %collective-permute-done.4.ac01_ref, ...), custom_call_target="tpu_custom_call" | custom-call | flops 1310720000 | bytes 6291456 | tf_op jit(solution)/shard_map/multiply/pallas_call | solution.py:73
  67.7 2.7 %collective-permute-start.8 = (f32[8,160,128]{2,1,0:T(8,128)S(1)}, f32[8,160,128]{2,1,0:T(8,128)S(1)}, u32[]{:S(2)}, u32[]{:S(2)}) collective-permute-start(f32[8,160,128]{2,1,0:T(8,128)S(1)} %multiply.3), channel_id=1, source_target_pairs={{0,32},{32,0},{1,33},{33,1},{2,34},{34,2},{3,35},{35,3},{4,36},{36... | collective-permute-start | bytes 1966088 | tf_op jit(solution)/shard_map/ppermute | solution.py:142
  70.3 3.5 %multiply.2 = f32[8,160,128]{2,1,0:T(8,128)S(1)} custom-call(s32[1]{0:T(128)} %bitcast.m_ref, bf16[16,32]{1,0:T(8,128)(2,1)S(1)} %reshape_squeeze.3.amp_ref, bf16[1600,128]{1,0:T(8,128)(2,1)S(1)} %collective-permute-done.3.ac00_ref, bf16[1600,128]{1,0:T(8,128)(2,1)S(1)} %collective-permute-done.4.ac01_ref, ...), custom_call_target="tpu_custom_call" | custom-call | flops 1310720000 | bytes 6291456 | tf_op jit(solution)/shard_map/multiply/pallas_call | solution.py:73
  73.8 0.0 collective-permute-done.8
  73.8 0.1 add_convert_fusion
  73.9 39.3 %all_to_all.10.parts_ref = bf16[8,160,128]{2,1,0:T(8,128)(2,1)} all-to-all(bf16[8,160,128]{2,1,0:T(8,128)(2,1)S(1)} %add_convert_fusion), channel_id=1, replica_groups=mesh['yl'=2,'x'=4,'core'=2,'zh'=8,'zp'=2,'yh'=2] {'zh'}, dimensions={0} | all-to-all | bytes 655360 | tf_op jit(solution)/shard_map/all_to_all | solution.py:143
  113.2 1.9 %finish.1 = f32[50,4,100]{2,1,0:T(4,128)} custom-call(bf16[8,160,128]{2,1,0:T(8,128)(2,1)} %all_to_all.10.parts_ref), custom_call_target="tpu_custom_call" | custom-call | tf_op jit(solution)/shard_map/finish/pallas_call | solution.py:99
  (5 shorter events, 0.1 us)
Async XLA Ops:
  1.1 12.2 %collective-permute-start.1 = (bf16[56,1024]{1,0:T(8,128)(2,1)S(1)}, bf16[56,1024]{1,0:T(8,128)(2,1)S(1)}, u32[]{:S(2)}, u32[]{:S(2)}) collective-permute-start(bf16[56,1024]{1,0:T(8,128)(2,1)S(1)} %pad.12), channel_id=1, source_target_pairs={{0,1},{1,0},{2,33},{3,32},{32,3},{33,2},{34,35},{35,34},{4,5},{5,4... | collective-permute-start | bytes 344072 | tf_op jit(solution)/shard_map/ppermute | solution.py:120
  6.2 7.0 %collective-permute-start = (bf16[56,1024]{1,0:T(8,128)(2,1)S(1)}, bf16[56,1024]{1,0:T(8,128)(2,1)S(1)}, u32[]{:S(2)}, u32[]{:S(2)}) collective-permute-start(bf16[56,1024]{1,0:T(8,128)(2,1)S(1)} %pad.11), channel_id=1, source_target_pairs={{0,0},{1,1},{2,32},{3,33},{32,2},{33,3},{34,34},{35,35},{4,4},{5,5... | collective-permute-start | bytes 344072 | tf_op jit(solution)/shard_map/ppermute | solution.py:120
  7.8 5.4 %collective-permute-start.2 = (bf16[32]{0:T(256)(128)(2,1)S(1)}, bf16[32]{0:T(256)(128)(2,1)S(1)}, u32[]{:S(2)}, u32[]{:S(2)}) collective-permute-start(bf16[32]{0:T(256)(128)(2,1)S(1)} %reshape.68), channel_id=1, source_target_pairs={{0,32},{32,0},{1,33},{33,1},{2,34},{34,2},{3,35},{35,3},{4,36},{36... | collective-permute-start | bytes 200 | tf_op jit(solution)/shard_map/ppermute | solution.py:133
  14.8 41.8 %all-to-all-start = ((bf16[8,2,56,1024]{3,2,1,0:T(8,128)(2,1)}), bf16[8,2,56,1024]{3,2,1,0:T(8,128)(2,1)S(1)}, u32[]{:S(2)}, u32[]{:S(2)}) async-start(bf16[8,2,56,1024]{3,2,1,0:T(8,128)(2,1)} %broadcast_in_dim.5), calls=%async_computation | async-start | bytes 3670016 | tf_op jit(solution)/shard_map/all_to_all | solution.py:136
  20.2 31.4 %collective-permute-start.5 = (bf16[1600,128]{1,0:T(8,128)(2,1)}, bf16[1600,128]{1,0:T(8,128)(2,1)}, u32[]{:S(2)}, u32[]{:S(2)}) collective-permute-start(bf16[1600,128]{1,0:T(8,128)(2,1)} %bitcast.7), channel_id=1, source_target_pairs={{0,1},{1,0},{2,3},{3,2},{32,33},{33,32},{34,35},{35,34},{4,5},{5,4... | collective-permute-start | bytes 1228808 | tf_op jit(solution)/shard_map/ppermute | solution.py:120
  24.0 32.7 %collective-permute-start.3 = (bf16[1600,128]{1,0:T(8,128)(2,1)}, bf16[1600,128]{1,0:T(8,128)(2,1)S(1)}, u32[]{:S(2)}, u32[]{:S(2)}) collective-permute-start(bf16[1600,128]{1,0:T(8,128)(2,1)} %bitcast.7), channel_id=1, source_target_pairs={{0,0},{1,1},{2,32},{3,33},{32,2},{33,3},{34,34},{35,35},{4,4},{5,5... | collective-permute-start | bytes 1228808 | tf_op jit(solution)/shard_map/ppermute | solution.py:120
  25.7 31.0 %collective-permute-start.4 = (bf16[1600,128]{1,0:T(8,128)(2,1)}, bf16[1600,128]{1,0:T(8,128)(2,1)S(1)}, u32[]{:S(2)}, u32[]{:S(2)}) collective-permute-start(bf16[1600,128]{1,0:T(8,128)(2,1)} %bitcast.7), channel_id=1, source_target_pairs={{0,2},{1,3},{2,34},{3,35},{32,0},{33,1},{34,32},{35,33},{4,6},{5,7... | collective-permute-start | bytes 1228808 | tf_op jit(solution)/shard_map/ppermute | solution.py:120
  51.6 5.1 %collective-permute-start.6 = (bf16[1600,128]{1,0:T(8,128)(2,1)}, bf16[1600,128]{1,0:T(8,128)(2,1)S(1)}, u32[]{:S(2)}, u32[]{:S(2)}) collective-permute-start(bf16[1600,128]{1,0:T(8,128)(2,1)} %collective-permute-done.5), channel_id=1, source_target_pairs={{0,0},{1,1},{2,32},{3,33},{32,2},{33,3},{34,34},{35,35},{4,4},{5,5... | collective-permute-start | bytes 1228808 | tf_op jit(solution)/shard_map/ppermute | solution.py:120
  53.3 10.9 %collective-permute-start.7 = (bf16[1600,128]{1,0:T(8,128)(2,1)}, bf16[1600,128]{1,0:T(8,128)(2,1)S(1)}, u32[]{:S(2)}, u32[]{:S(2)}) collective-permute-start(bf16[1600,128]{1,0:T(8,128)(2,1)} %collective-permute-done.5), channel_id=1, source_target_pairs={{0,2},{1,3},{2,34},{3,35},{32,0},{33,1},{34,32},{35,33},{4,6},{5,7... | collective-permute-start | bytes 1228808 | tf_op jit(solution)/shard_map/ppermute | solution.py:120
  67.7 6.1 %collective-permute-start.8 = (f32[8,160,128]{2,1,0:T(8,128)S(1)}, f32[8,160,128]{2,1,0:T(8,128)S(1)}, u32[]{:S(2)}, u32[]{:S(2)}) collective-permute-start(f32[8,160,128]{2,1,0:T(8,128)S(1)} %multiply.3), channel_id=1, source_target_pairs={{0,32},{32,0},{1,33},{33,1},{2,34},{34,2},{3,35},{35,3},{4,36},{36... | collective-permute-start | bytes 1966088 | tf_op jit(solution)/shard_map/ppermute | solution.py:142

commit v3 on v2

--- a/solution.py
+++ b/solution.py
@@ -13,8 +13,8 @@
 NA, NB, C, D, NP, Q = 100, 100, 16, 8, 4, 128
 ROWS = NA * NP
 HALF = 50
-UNIT = 56
-PAD = 64
+UNIT = 104
+WIDE = 128
 PIECE = 160
 
 
@@ -33,6 +33,30 @@
     return jnp.where(row % wide == col // C, full, 0.0).astype(jnp.bfloat16)
 
 
+def unit_kernel(one_ref, two_ref, amp_ref, later_ref, out_ref, unit_ref, sem_ref):
+    unit_ref[0:HALF, :] = one_ref[...]
+    unit_ref[HALF:2 * HALF, :] = two_ref[...]
+    unit_ref[2 * HALF:, :] = jnp.zeros((UNIT - 2 * HALF, D * Q), jnp.bfloat16)
+    unit_ref[2 * HALF:2 * HALF + 1, 0:2 * D * NP] = amp_ref[...]
+    copies = [pltpu.make_async_copy(unit_ref, out_ref.at[t], sem_ref.at[t]) for t in range(8)]
+    for copy in copies:
+        copy.start()
+    for copy in copies:
+        copy.wait()
+
+
+def make_unit(one, two, amp, later):
+    inside, outside = pl.BlockSpec(memory_space=pltpu.VMEM), pl.BlockSpec(memory_space=pl.ANY)
+    return pl.pallas_call(
+        unit_kernel,
+        in_specs=[inside, inside, inside, outside],
+        out_specs=outside,
+        out_shape=jax.ShapeDtypeStruct((8, UNIT, D * Q), jnp.bfloat16),
+        scratch_shapes=[pltpu.VMEM((UNIT, D * Q), jnp.bfloat16), pltpu.SemaphoreType.DMA((8,))],
+        name="make_unit",
+    )(one, two, amp, later)
+
+
 def product_kernel(m_ref, amp_ref, ac00_ref, ac01_ref, ac10_ref, ac11_ref, bd_ref, out_ref, ac_ref, x_ref, left_ref, acc_ref):
     for m, pair in enumerate(((ac00_ref, ac10_ref), (ac01_ref, ac11_ref))):
 
@@ -43,29 +67,31 @@
 
     for dy in range(2):
         for t in range(8):
-            left_ref[t, 0:UNIT, dy * D * Q:(dy + 1) * D * Q] = bd_ref[t, dy]
+            left_ref[HALF * t:HALF * (t + 1), dy * D * Q:(dy + 1) * D * Q] = bd_ref[t, HALF * dy:HALF * (dy + 1), :]
     w16, w4 = spread(amp_ref[...], 16), spread(amp_ref[...], 4)
     for k in range(7):
         w, n = (w16, 16) if k < 6 else (w4, 4)
         y = jnp.dot(w, ac_ref[k * 256:k * 256 + n * C, :], preferred_element_type=jnp.float32)
         high = y.astype(jnp.bfloat16)
         low = (y - high.astype(jnp.float32)).astype(jnp.bfloat16)
-        tall = NP * n
         for dy in range(2):
             for d in range(D):
-                rows, columns = slice(64 * k, 64 * k + tall), slice((dy * D + d) * Q, (dy * D + d + 1) * Q)
-                here = slice(tall * d, tall * (d + 1)), slice(Q * dy, Q * (dy + 1))
-                x_ref[0, rows, columns] = high[here]
-                x_ref[1, rows, columns] = low[here]
-    left = left_ref[...].reshape(8 * PAD, 2 * D * Q)
-    acc_ref[...] = lax.dot_general(left, x_ref[0], NT, preferred_element_type=jnp.float32) + lax.dot_general(
-        left, x_ref[1], NT, preferred_element_type=jnp.float32
+                for p in range(NP):
+                    rows, columns = slice(WIDE * p + 16 * k, WIDE * p + 16 * k + n), slice((dy * D + d) * Q, (dy * D + d + 1) * Q)
+                    here = slice(n * (d * NP + p), n * (d * NP + p + 1)), slice(Q * dy, Q * (dy + 1))
+                    x_ref[0, rows, columns] = high[here]
+                    x_ref[1, rows, columns] = low[here]
+    acc_ref[...] = lax.dot_general(left_ref[...], x_ref[0], NT, preferred_element_type=jnp.float32) + lax.dot_general(
+        left_ref[...], x_ref[1], NT, preferred_element_type=jnp.float32
     )
     for t in range(8):
-        at = t * PAD
+        at = slice(HALF * t, HALF * (t + 1))
+        last = acc_ref[at, 3 * WIDE:3 * WIDE + NA]
         for j in range(3):
-            out_ref[t, 50 * j:50 * j + 50, :] = acc_ref[at:at + 50, 128 * j:128 * (j + 1)]
-        rest = [acc_ref[at + 10 * g:at + 10 * g + 10, 384:400] for g in range(5)]
+            out_ref[t, 50 * j:50 * j + 50, :] = jnp.concatenate(
+                [acc_ref[at, WIDE * j:WIDE * j + NA], last[:, 28 * j:28 * j + 28]], axis=1
+            )
+        rest = [last[10 * g:10 * g + 10, 84:100] for g in range(5)]
         out_ref[t, 150:160, :] = jnp.concatenate(rest + [jnp.zeros((10, 48), jnp.float32)], axis=1)
 
 
@@ -76,9 +102,9 @@
         out_specs=pl.BlockSpec(memory_space=pltpu.VMEM),
         scratch_shapes=[
             pltpu.VMEM((NA * C, 2 * Q), jnp.bfloat16),
-            pltpu.VMEM((2, ROWS, 2 * D * Q), jnp.bfloat16),
-            pltpu.VMEM((8, PAD, 2 * D * Q), jnp.bfloat16),
-            pltpu.VMEM((8 * PAD, ROWS), jnp.float32),
+            pltpu.VMEM((2, NP * WIDE, 2 * D * Q), jnp.bfloat16),
+            pltpu.VMEM((8 * HALF, 2 * D * Q), jnp.bfloat16),
+            pltpu.VMEM((8 * HALF, NP * WIDE), jnp.float32),
         ],
         out_shape=jax.ShapeDtypeStruct((8, PIECE, 128), jnp.float32),
         compiler_params=pltpu.CompilerParams(vmem_limit_bytes=32 * MIB),
@@ -89,10 +115,10 @@
 
 def last_kernel(parts_ref, out_ref, sum_ref):
     sum_ref[...] = jnp.sum(parts_ref[...].astype(jnp.float32), axis=0)
+    for j in range(3):
+        out_ref[:, j, :] = sum_ref[50 * j:50 * j + 50, 0:NA]
     rest = jnp.concatenate([sum_ref[150:160, 16 * g:16 * (g + 1)] for g in range(5)], axis=0)
-    for p in range(NP):
-        pieces = [sum_ref[50 * (k // 2):50 * (k // 2) + 50, 64 * (k % 2) + 16 * p:64 * (k % 2) + 16 * p + 16] for k in range(6)]
-        out_ref[:, p, :] = jnp.concatenate(pieces + [rest[:, 4 * p:4 * p + 4]], axis=1)
+    out_ref[:, 3, :] = jnp.concatenate([sum_ref[50 * j:50 * j + 50, NA:] for j in range(3)] + [rest], axis=1)
 
 
 def finish(parts):
@@ -127,14 +153,12 @@
     units = []
     for dy in range(2):
         half = lax.dynamic_index_in_dim(halves, yh ^ dy, 0, keepdims=False)
-        half = jnp.pad(half, ((0, UNIT - HALF), (0, 0)))
         units.append(sent(half, lambda e, z, y: (z, e, y ^ dy)))
-    flat = jnp.transpose(amplitudes, (1, 2, 0)).reshape(D * NP)
+    flat = jnp.transpose(amplitudes, (1, 2, 0)).reshape(1, D * NP)
     peer = lax.ppermute(flat, "core", [(0, 1), (1, 0)])
-    two = jnp.where(core == 0, jnp.concatenate([flat, peer]), jnp.concatenate([peer, flat]))
-    both = jnp.stack(units) + jnp.pad(two[None, None], ((0, 1), (HALF, UNIT - HALF - 1), (0, D * Q - 2 * D * NP)))
-    bd = lax.all_to_all(jnp.broadcast_to(both[None], (8,) + both.shape), ("yl", "x"), 0, 0, tiled=True)
-    amp = bd[:, 0, HALF, :2 * D * NP].reshape(C, D * NP)
+    two = jnp.where(core == 0, jnp.concatenate([flat, peer], axis=1), jnp.concatenate([peer, flat], axis=1))
+    bd = lax.all_to_all(make_unit(*units, two, across), ("yl", "x"), 0, 0, tiled=True)
+    amp = bd[:, 2 * HALF, :2 * D * NP].reshape(C, D * NP)
 
     m = (zp ^ core).astype(jnp.int32)[None]
     for_other = multiply(m ^ 1, amp, blocks, bd)

time: 116 us -> 101 us (0.87)
  the two profiles are of different devices: /device:TPU:2 before, /device:TPU:1 now
where the time goes in v3:
time: 101 us; the launch traced here: 100 us
  blocking collectives  39.4 us (39%)
  starting transfers between devices  32.6 us (32%)
  waiting for transfers between devices  14.1 us (14%)
  Pallas kernels  10.3 us (10%)
  local copies, waits for them, and re-layouts  2.68 us (3%)
    all_to_all x1, blocking collectives, on_device(): summed = finish(lax.all_to_all(pieces, 'zh', 0, 0, tiled=True))  39.4 us
    ppermute x7, starting transfers between devices, sent(): return lax.ppermute(array, group, ways)  21.5 us
    all_to_all x1, waiting for transfers between devices, on_device(): lax.all_to_all(make_unit(*units, two, across), ('yl', 'x'), 0, 0, tiled=T...  13.3 us
    pallas_call x2, Pallas kernels, multiply(): pl.pallas_call(product_kernel, in_specs=[pl.BlockSpec(memory_space=pltpu....  6.28 us
    ppermute x1, starting transfers between devices, on_device(): peer = lax.ppermute(flat, 'core', [(0, 1), (1, 0)])  4.83 us
    all_to_all x1, starting transfers between devices, on_device(): lax.all_to_all(make_unit(*units, two, across), ('yl', 'x'), 0, 0, tiled=T...  3.6 us
    ppermute x1, starting transfers between devices, on_device(): lax.ppermute(for_other, 'core', [(0, 1), (1, 0)])  2.7 us
    pallas_call x1, Pallas kernels, make_unit(): pl.pallas_call(unit_kernel, in_specs=[inside, inside, inside, outside], o...  2.27 us
  transfers between devices with their start and end apart: 10, of which 2 were waited for; matrix products, arithmetic and copies ran while one was open for 3% of the time, Pallas kernels for 3%

profile of v3, /device:TPU:1, one launch (start us, length us, event | category | flops | bytes accessed | tf_op | source)
XLA Modules:
  0.0 100.0 jit_solution(6064546557893818578)
XLA Ops:
  0.0 5.6 %collective-permute-start.3 = (bf16[1600,128]{1,0:T(8,128)(2,1)}, bf16[1600,128]{1,0:T(8,128)(2,1)}, u32[]{:S(2)}, u32[]{:S(2)}) collective-permute-start(bf16[1600,128]{1,0:T(8,128)(2,1)} %bitcast.4), channel_id=1, source_target_pairs={{0,1},{1,0},{2,3},{3,2},{32,33},{33,32},{34,35},{35,34},{4,5},{5,4... | collective-permute-start | bytes 1228808 | tf_op jit(solution)/shard_map/ppermute | solution.py:146
  5.7 1.0 %reshape.67 = bf16[2,50,1024]{2,1,0:T(8,128)(2,1)S(1)} reshape(bf16[100,8,128]{2,1,0:T(8,128)(2,1)} %param.4) | data formatting | bytes 409600 | tf_op jit(solution)/shard_map/reshape | solution.py:152
  6.7 4.4 %collective-permute-start = (bf16[50,1024]{1,0:T(8,128)(2,1)S(1)}, bf16[50,1024]{1,0:T(8,128)(2,1)S(1)}, u32[]{:S(2)}, u32[]{:S(2)}) collective-permute-start(bf16[50,1024]{1,0:T(8,128)(2,1)S(1)} %get-tuple-element.6), channel_id=1, source_target_pairs={{0,0},{1,1},{2,32},{3,33},{32,2},{33,3},{34,34},{35,35},{4,4},{5,5... | collective-permute-start | bytes 307208 | tf_op jit(solution)/shard_map/ppermute | solution.py:146
  11.1 1.9 %collective-permute-start.1 = (bf16[50,1024]{1,0:T(8,128)(2,1)S(1)}, bf16[50,1024]{1,0:T(8,128)(2,1)S(1)}, u32[]{:S(2)}, u32[]{:S(2)}) collective-permute-start(bf16[50,1024]{1,0:T(8,128)(2,1)S(1)} %get-tuple-element.5), channel_id=1, source_target_pairs={{0,1},{1,0},{2,33},{3,32},{32,3},{33,2},{34,35},{35,34},{4,5},{5,4... | collective-permute-start | bytes 307208 | tf_op jit(solution)/shard_map/ppermute | solution.py:146
  13.1 0.8 copy.5
  13.8 0.1 concatenate.24
  13.9 4.8 %collective-permute-start.2 = (bf16[1,32]{1,0:T(2,128)(2,1)S(1)}, bf16[1,32]{1,0:T(2,128)(2,1)S(1)}, u32[]{:S(2)}, u32[]{:S(2)}) collective-permute-start(bf16[1,32]{1,0:T(2,128)(2,1)S(1)} %concatenate.24), channel_id=1, source_target_pairs={{0,32},{32,0},{1,33},{33,1},{2,34},{34,2},{3,35},{35,3},{4,36},{36... | collective-permute-start | bytes 200 | tf_op jit(solution)/shard_map/ppermute | solution.py:158
  18.8 0.8 collective-permute-done.2
  19.6 0.6 broadcast_select_fusion.amp_ref
  20.1 0.0 collective-permute-done.one_ref
  20.1 0.0 copy-start
  20.2 0.0 collective-permute-done.1.two_ref
  20.2 0.0 copy-start.1
  20.2 0.0 collective-permute-done.3.later_ref
  20.2 0.6 copy-done
  20.8 0.0 copy-done.1
  20.8 2.3 %make_unit.1 = bf16[8,104,1024]{2,1,0:T(8,128)(2,1)} custom-call(bf16[50,1024]{1,0:T(8,128)(2,1)} %copy-done, bf16[50,1024]{1,0:T(8,128)(2,1)} %copy-done.1, bf16[1,64]{1,0:T(2,128)(2,1)} %broadcast_select_fusion.amp_ref, bf16[1600,128]{1,0:T(8,128)(2,1)} %collective-permute-done.3.later_ref), custom_call_target="tpu_custom_call" | custom-call | tf_op jit(solution)/shard_map/make_unit/pallas_call | solution.py:50
  23.1 3.6 %all-to-all-start = ((bf16[8,104,1024]{2,1,0:T(8,128)(2,1)}), bf16[8,104,1024]{2,1,0:T(8,128)(2,1)S(1)}, u32[]{:S(2)}, u32[]{:S(2)}) async-start(bf16[8,104,1024]{2,1,0:T(8,128)(2,1)} %make_unit.1), calls=%async_computation | async-start | bytes 3407872 | tf_op jit(solution)/shard_map/all_to_all | solution.py:160
  26.7 3.1 %collective-permute-start.4 = (bf16[1600,128]{1,0:T(8,128)(2,1)}, bf16[1600,128]{1,0:T(8,128)(2,1)S(1)}, u32[]{:S(2)}, u32[]{:S(2)}) collective-permute-start(bf16[1600,128]{1,0:T(8,128)(2,1)} %bitcast.4), channel_id=1, source_target_pairs={{0,0},{1,1},{2,32},{3,33},{32,2},{33,3},{34,34},{35,35},{4,4},{5,5... | collective-permute-start | bytes 1228808 | tf_op jit(solution)/shard_map/ppermute | solution.py:146
  29.8 1.9 %collective-permute-start.5 = (bf16[1600,128]{1,0:T(8,128)(2,1)}, bf16[1600,128]{1,0:T(8,128)(2,1)S(1)}, u32[]{:S(2)}, u32[]{:S(2)}) collective-permute-start(bf16[1600,128]{1,0:T(8,128)(2,1)} %bitcast.4), channel_id=1, source_target_pairs={{0,2},{1,3},{2,34},{3,35},{32,0},{33,1},{34,32},{35,33},{4,6},{5,7... | collective-permute-start | bytes 1228808 | tf_op jit(solution)/shard_map/ppermute | solution.py:146
  31.8 2.5 %collective-permute-start.6 = (bf16[1600,128]{1,0:T(8,128)(2,1)}, bf16[1600,128]{1,0:T(8,128)(2,1)S(1)}, u32[]{:S(2)}, u32[]{:S(2)}) collective-permute-start(bf16[1600,128]{1,0:T(8,128)(2,1)} %collective-permute-done.3.later_ref), channel_id=1, source_target_pairs={{0,0},{1,1},{2,32},{3,33},{32,2},{33,3},{34,34},{35,35},{4,4},{5,5... | collective-permute-start | bytes 1228808 | tf_op jit(solution)/shard_map/ppermute | solution.py:146
  34.2 2.0 %collective-permute-start.7 = (bf16[1600,128]{1,0:T(8,128)(2,1)}, bf16[1600,128]{1,0:T(8,128)(2,1)S(1)}, u32[]{:S(2)}, u32[]{:S(2)}) collective-permute-start(bf16[1600,128]{1,0:T(8,128)(2,1)} %collective-permute-done.3.later_ref), channel_id=1, source_target_pairs={{0,2},{1,3},{2,34},{3,35},{32,0},{33,1},{34,32},{35,33},{4,6},{5,7... | collective-permute-start | bytes 1228808 | tf_op jit(solution)/shard_map/ppermute | solution.py:146
  36.3 13.3 %all-to-all-done.bd_ref = bf16[8,104,1024]{2,1,0:T(8,128)(2,1)S(1)} async-done(((bf16[8,104,1024]{2,1,0:T(8,128)(2,1)}), bf16[8,104,1024]{2,1,0:T(8,128)(2,1)S(1)}, u32[]{:S(2)}, u32[]{:S(2)}) %all-to-all-start) | async-done | bytes 1703968 | tf_op jit(solution)/shard_map/all_to_all | solution.py:160
  49.6 0.1 reshape_squeeze.3.amp_ref
  49.7 0.0 collective-permute-done.4.ac00_ref
  49.7 0.0 collective-permute-done.5.ac01_ref
  49.7 0.0 collective-permute-done.6.ac10_ref
  49.7 0.0 collective-permute-done.7.ac11_ref
  49.7 3.1 %multiply.3 = f32[8,160,128]{2,1,0:T(8,128)S(1)} custom-call(s32[1]{0:T(128)S(6)} %xor.11.m_ref, bf16[16,32]{1,0:T(8,128)(2,1)S(1)} %reshape_squeeze.3.amp_ref, bf16[1600,128]{1,0:T(8,128)(2,1)S(1)} %collective-permute-done.4.ac00_ref, bf16[1600,128]{1,0:T(8,128)(2,1)S(1)} %collective-permute-done.5.ac01_ref, ...), custom_call_target="tpu_custom_call" | custom-call | flops 1310720000 | bytes 6291456 | tf_op jit(solution)/shard_map/multiply/pallas_call | solution.py:99
  52.9 2.7 %collective-permute-start.8 = (f32[8,160,128]{2,1,0:T(8,128)S(1)}, f32[8,160,128]{2,1,0:T(8,128)S(1)}, u32[]{:S(2)}, u32[]{:S(2)}) collective-permute-start(f32[8,160,128]{2,1,0:T(8,128)S(1)} %multiply.3), channel_id=1, source_target_pairs={{0,32},{32,0},{1,33},{33,1},{2,34},{34,2},{3,35},{35,3},{4,36},{36... | collective-permute-start | bytes 1966088 | tf_op jit(solution)/shard_map/ppermute | solution.py:166
  55.6 3.1 %multiply.2 = f32[8,160,128]{2,1,0:T(8,128)S(1)} custom-call(s32[1]{0:T(128)} %bitcast.m_ref, bf16[16,32]{1,0:T(8,128)(2,1)S(1)} %reshape_squeeze.3.amp_ref, bf16[1600,128]{1,0:T(8,128)(2,1)S(1)} %collective-permute-done.4.ac00_ref, bf16[1600,128]{1,0:T(8,128)(2,1)S(1)} %collective-permute-done.5.ac01_ref, ...), custom_call_target="tpu_custom_call" | custom-call | flops 1310720000 | bytes 6291456 | tf_op jit(solution)/shard_map/multiply/pallas_call | solution.py:99
  58.7 0.0 collective-permute-done.8
  58.7 0.1 add_convert_fusion
  58.8 39.4 %all_to_all.10.parts_ref = bf16[8,160,128]{2,1,0:T(8,128)(2,1)} all-to-all(bf16[8,160,128]{2,1,0:T(8,128)(2,1)S(1)} %add_convert_fusion), channel_id=1, replica_groups=mesh['yl'=2,'x'=4,'core'=2,'zh'=8,'zp'=2,'yh'=2] {'zh'}, dimensions={0} | all-to-all | bytes 655360 | tf_op jit(solution)/shard_map/all_to_all | solution.py:167
  98.2 1.8 %finish.1 = f32[50,4,100]{2,1,0:T(4,128)} custom-call(bf16[8,160,128]{2,1,0:T(8,128)(2,1)} %all_to_all.10.parts_ref), custom_call_target="tpu_custom_call" | custom-call | tf_op jit(solution)/shard_map/finish/pallas_call | solution.py:125
  (2 shorter events, 0.1 us)
Async XLA Ops:
  0.0 20.2 %collective-permute-start.3 = (bf16[1600,128]{1,0:T(8,128)(2,1)}, bf16[1600,128]{1,0:T(8,128)(2,1)}, u32[]{:S(2)}, u32[]{:S(2)}) collective-permute-start(bf16[1600,128]{1,0:T(8,128)(2,1)} %bitcast.4), channel_id=1, source_target_pairs={{0,1},{1,0},{2,3},{3,2},{32,33},{33,32},{34,35},{35,34},{4,5},{5,4... | collective-permute-start | bytes 1228808 | tf_op jit(solution)/shard_map/ppermute | solution.py:146
  6.7 13.4 %collective-permute-start = (bf16[50,1024]{1,0:T(8,128)(2,1)S(1)}, bf16[50,1024]{1,0:T(8,128)(2,1)S(1)}, u32[]{:S(2)}, u32[]{:S(2)}) collective-permute-start(bf16[50,1024]{1,0:T(8,128)(2,1)S(1)} %get-tuple-element.6), channel_id=1, source_target_pairs={{0,0},{1,1},{2,32},{3,33},{32,2},{33,3},{34,34},{35,35},{4,4},{5,5... | collective-permute-start | bytes 307208 | tf_op jit(solution)/shard_map/ppermute | solution.py:146
  11.1 9.0 %collective-permute-start.1 = (bf16[50,1024]{1,0:T(8,128)(2,1)S(1)}, bf16[50,1024]{1,0:T(8,128)(2,1)S(1)}, u32[]{:S(2)}, u32[]{:S(2)}) collective-permute-start(bf16[50,1024]{1,0:T(8,128)(2,1)S(1)} %get-tuple-element.5), channel_id=1, source_target_pairs={{0,1},{1,0},{2,33},{3,32},{32,3},{33,2},{34,35},{35,34},{4,5},{5,4... | collective-permute-start | bytes 307208 | tf_op jit(solution)/shard_map/ppermute | solution.py:146
  13.9 5.6 %collective-permute-start.2 = (bf16[1,32]{1,0:T(2,128)(2,1)S(1)}, bf16[1,32]{1,0:T(2,128)(2,1)S(1)}, u32[]{:S(2)}, u32[]{:S(2)}) collective-permute-start(bf16[1,32]{1,0:T(2,128)(2,1)S(1)} %concatenate.24), channel_id=1, source_target_pairs={{0,32},{32,0},{1,33},{33,1},{2,34},{34,2},{3,35},{35,3},{4,36},{36... | collective-permute-start | bytes 200 | tf_op jit(solution)/shard_map/ppermute | solution.py:158
  20.1 0.6 copy-start
  20.2 0.7 copy-start.1
  23.1 26.5 %all-to-all-start = ((bf16[8,104,1024]{2,1,0:T(8,128)(2,1)}), bf16[8,104,1024]{2,1,0:T(8,128)(2,1)S(1)}, u32[]{:S(2)}, u32[]{:S(2)}) async-start(bf16[8,104,1024]{2,1,0:T(8,128)(2,1)} %make_unit.1), calls=%async_computation | async-start | bytes 3407872 | tf_op jit(solution)/shard_map/all_to_all | solution.py:160
  26.7 23.0 %collective-permute-start.4 = (bf16[1600,128]{1,0:T(8,128)(2,1)}, bf16[1600,128]{1,0:T(8,128)(2,1)S(1)}, u32[]{:S(2)}, u32[]{:S(2)}) collective-permute-start(bf16[1600,128]{1,0:T(8,128)(2,1)} %bitcast.4), channel_id=1, source_target_pairs={{0,0},{1,1},{2,32},{3,33},{32,2},{33,3},{34,34},{35,35},{4,4},{5,5... | collective-permute-start | bytes 1228808 | tf_op jit(solution)/shard_map/ppermute | solution.py:146
  29.8 19.9 %collective-permute-start.5 = (bf16[1600,128]{1,0:T(8,128)(2,1)}, bf16[1600,128]{1,0:T(8,128)(2,1)S(1)}, u32[]{:S(2)}, u32[]{:S(2)}) collective-permute-start(bf16[1600,128]{1,0:T(8,128)(2,1)} %bitcast.4), channel_id=1, source_target_pairs={{0,2},{1,3},{2,34},{3,35},{32,0},{33,1},{34,32},{35,33},{4,6},{5,7... | collective-permute-start | bytes 1228808 | tf_op jit(solution)/shard_map/ppermute | solution.py:146
  31.8 17.9 %collective-permute-start.6 = (bf16[1600,128]{1,0:T(8,128)(2,1)}, bf16[1600,128]{1,0:T(8,128)(2,1)S(1)}, u32[]{:S(2)}, u32[]{:S(2)}) collective-permute-start(bf16[1600,128]{1,0:T(8,128)(2,1)} %collective-permute-done.3.later_ref), channel_id=1, source_target_pairs={{0,0},{1,1},{2,32},{3,33},{32,2},{33,3},{34,34},{35,35},{4,4},{5,5... | collective-permute-start | bytes 1228808 | tf_op jit(solution)/shard_map/ppermute | solution.py:146
  34.2 15.5 %collective-permute-start.7 = (bf16[1600,128]{1,0:T(8,128)(2,1)}, bf16[1600,128]{1,0:T(8,128)(2,1)S(1)}, u32[]{:S(2)}, u32[]{:S(2)}) collective-permute-start(bf16[1600,128]{1,0:T(8,128)(2,1)} %collective-permute-done.3.later_ref), channel_id=1, source_target_pairs={{0,2},{1,3},{2,34},{3,35},{32,0},{33,1},{34,32},{35,33},{4,6},{5,7... | collective-permute-start | bytes 1228808 | tf_op jit(solution)/shard_map/ppermute | solution.py:146
  52.9 5.9 %collective-permute-start.8 = (f32[8,160,128]{2,1,0:T(8,128)S(1)}, f32[8,160,128]{2,1,0:T(8,128)S(1)}, u32[]{:S(2)}, u32[]{:S(2)}) collective-permute-start(f32[8,160,128]{2,1,0:T(8,128)S(1)} %multiply.3), channel_id=1, source_target_pairs={{0,32},{32,0},{1,33},{33,1},{2,34},{34,2},{3,35},{35,3},{4,36},{36... | collective-permute-start | bytes 1966088 | tf_op jit(solution)/shard_map/ppermute | solution.py:166

commit v4 on v3

--- a/solution.py
+++ b/solution.py
@@ -5,8 +5,10 @@
 from jax.experimental.pallas import tpu as pltpu
 from jax.sharding import Mesh, PartitionSpec as P
 
-ROW = ("yl", "x", "core")
-COL = ("zh", "zp", "yh")
+ROW = ("yl", "xh", "xl", "core")
+COL = ("zq", "zl", "yh")
+DELTA = ((2, 1), (0, 3))
+HALF_OF = (1, 0, 0, 1)
 NT = (((1,), (1,)), ((), ()))
 MIB = 1024 * 1024
 
@@ -33,11 +35,25 @@
     return jnp.where(row % wide == col // C, full, 0.0).astype(jnp.bfloat16)
 
 
-def unit_kernel(one_ref, two_ref, amp_ref, later_ref, out_ref, unit_ref, sem_ref):
-    unit_ref[0:HALF, :] = one_ref[...]
-    unit_ref[HALF:2 * HALF, :] = two_ref[...]
-    unit_ref[2 * HALF:, :] = jnp.zeros((UNIT - 2 * HALF, D * Q), jnp.bfloat16)
-    unit_ref[2 * HALF:2 * HALF + 1, 0:2 * D * NP] = amp_ref[...]
+def in_a_row(amp):
+    row = lax.broadcasted_iota(jnp.int32, (D, D * NP), 0)
+    col = lax.broadcasted_iota(jnp.int32, (D, D * NP), 1)
+    pick = jnp.where(col // NP == row, 1.0, 0.0).astype(jnp.bfloat16)
+    wide = jnp.dot(amp, pick, preferred_element_type=jnp.float32)
+    row = lax.broadcasted_iota(jnp.int32, (NP, D * NP), 0)
+    col = lax.broadcasted_iota(jnp.int32, (NP, D * NP), 1)
+    return jnp.sum(jnp.where(col % NP == row, wide, 0.0), axis=0, keepdims=True)
+
+
+def unit_kernel(core_ref, bd_ref, amp_ref, peer_ref, out_ref, wide_ref, unit_ref, sem_ref):
+    wide_ref[...] = bd_ref[...].astype(jnp.float32).reshape(NB * D, Q)
+    for d in range(D):
+        unit_ref[0:NB, d * Q:(d + 1) * Q] = wide_ref[pl.ds(d, NB, stride=D), :].astype(jnp.bfloat16)
+    unit_ref[NB:, :] = jnp.zeros((UNIT - NB, D * Q), jnp.bfloat16)
+    own, peer = in_a_row(amp_ref[...]), in_a_row(peer_ref[...])
+    first = core_ref[0] == 0
+    both = jnp.concatenate([jnp.where(first, own, peer), jnp.where(first, peer, own)], axis=1)
+    unit_ref[NB:NB + 1, 0:2 * D * NP] = both.astype(jnp.bfloat16)
     copies = [pltpu.make_async_copy(unit_ref, out_ref.at[t], sem_ref.at[t]) for t in range(8)]
     for copy in copies:
         copy.start()
@@ -45,16 +61,21 @@
         copy.wait()
 
 
-def make_unit(one, two, amp, later):
+def make_unit(core, bd, amp, peer):
     inside, outside = pl.BlockSpec(memory_space=pltpu.VMEM), pl.BlockSpec(memory_space=pl.ANY)
     return pl.pallas_call(
         unit_kernel,
-        in_specs=[inside, inside, inside, outside],
+        in_specs=[pl.BlockSpec(memory_space=pltpu.SMEM), inside, inside, inside],
         out_specs=outside,
         out_shape=jax.ShapeDtypeStruct((8, UNIT, D * Q), jnp.bfloat16),
-        scratch_shapes=[pltpu.VMEM((UNIT, D * Q), jnp.bfloat16), pltpu.SemaphoreType.DMA((8,))],
+        scratch_shapes=[
+            pltpu.VMEM((NB * D, Q), jnp.float32),
+            pltpu.VMEM((UNIT, D * Q), jnp.bfloat16),
+            pltpu.SemaphoreType.DMA((8,)),
+        ],
+        compiler_params=pltpu.CompilerParams(vmem_limit_bytes=16 * MIB),
         name="make_unit",
-    )(one, two, amp, later)
+    )(core, bd, amp, peer)
 
 
 def product_kernel(m_ref, amp_ref, ac00_ref, ac01_ref, ac10_ref, ac11_ref, bd_ref, out_ref, ac_ref, x_ref, left_ref, acc_ref):
@@ -62,23 +83,23 @@
 
         @pl.when(m_ref[0] == m)
         def _():
-            for dy in range(2):
-                ac_ref[:, dy * Q:(dy + 1) * Q] = pair[dy][...]
+            for h in range(2):
+                ac_ref[:, h * Q:(h + 1) * Q] = pair[h][...]
 
-    for dy in range(2):
-        for t in range(8):
-            left_ref[HALF * t:HALF * (t + 1), dy * D * Q:(dy + 1) * D * Q] = bd_ref[t, HALF * dy:HALF * (dy + 1), :]
+    for h in range(2):
+        for t in range(4):
+            left_ref[NB * t:NB * (t + 1), h * D * Q:(h + 1) * D * Q] = bd_ref[2 * t + h, 0:NB, :]
     w16, w4 = spread(amp_ref[...], 16), spread(amp_ref[...], 4)
     for k in range(7):
         w, n = (w16, 16) if k < 6 else (w4, 4)
         y = jnp.dot(w, ac_ref[k * 256:k * 256 + n * C, :], preferred_element_type=jnp.float32)
         high = y.astype(jnp.bfloat16)
         low = (y - high.astype(jnp.float32)).astype(jnp.bfloat16)
-        for dy in range(2):
+        for h in range(2):
             for d in range(D):
                 for p in range(NP):
-                    rows, columns = slice(WIDE * p + 16 * k, WIDE * p + 16 * k + n), slice((dy * D + d) * Q, (dy * D + d + 1) * Q)
-                    here = slice(n * (d * NP + p), n * (d * NP + p + 1)), slice(Q * dy, Q * (dy + 1))
+                    rows, columns = slice(WIDE * p + 16 * k, WIDE * p + 16 * k + n), slice((h * D + d) * Q, (h * D + d + 1) * Q)
+                    here = slice(n * (d * NP + p), n * (d * NP + p + 1)), slice(Q * h, Q * (h + 1))
                     x_ref[0, rows, columns] = high[here]
                     x_ref[1, rows, columns] = low[here]
     acc_ref[...] = lax.dot_general(left_ref[...], x_ref[0], NT, preferred_element_type=jnp.float32) + lax.dot_general(
@@ -128,48 +149,46 @@
         out_specs=pl.BlockSpec(memory_space=pltpu.VMEM),
         out_shape=jax.ShapeDtypeStruct((50, NP, NA), jnp.float32),
         scratch_shapes=[pltpu.VMEM((PIECE, 128), jnp.float32)],
+        compiler_params=pltpu.CompilerParams(vmem_limit_bytes=16 * MIB),
         name="finish",
     )(parts)
 
 
+def home(z, delta):
+    two = 2 if (z - delta) % 2 == 0 else -2
+    return (z - (0, 1, two, -1)[delta]) % 16
+
+
 def on_device(fitted_ac, fitted_bd, amplitudes):
-    core, zp, yh = (lax.axis_index(name) for name in ("core", "zp", "yh"))
-    group = ("core", "zp", "yh")
+    core, zl = (lax.axis_index(name) for name in ("core", "zl"))
+    ways = []
+    for f in range(4):
+        for z in range(16):
+            delta = (z - f) % 4
+            ways.append((16 * f + z, 32 * HALF_OF[delta] + 16 * (z % 2) + home(z, delta)))
+    shard = lax.ppermute(fitted_bd, ("xl", "core", "zq", "zl"), ways)
+    amp = amplitudes.reshape(NP, D)
+    peer = lax.ppermute(amp, "core", [(0, 1), (1, 0)])
+    bd = lax.all_to_all(make_unit(core.astype(jnp.int32)[None], shard, amp, peer), ("yl", "xh", "xl"), 0, 0, tiled=True)
+    ac = fitted_ac.reshape(NA * C, Q)
+    blocks = {}
+    for h in range(2):
+        for m in range(2):
+            ways = [(16 * e + z, 16 * (z % 2) + home(z, DELTA[h][e ^ m])) for e in range(2) for z in range(16)]
+            blocks[h, m] = lax.ppermute(ac, ("core", "zq", "zl"), ways)
+    blocks = [blocks[h, m] for h in range(2) for m in range(2)]
+    amp = bd[:, NB, :2 * D * NP].reshape(C, D * NP)
 
-    def sent(array, place):
-        ways = []
-        for e in range(2):
-            for z in range(2):
-                for y in range(2):
-                    to = place(e, z, y)
-                    ways.append((4 * e + 2 * z + y, 4 * to[0] + 2 * to[1] + to[2]))
-        return lax.ppermute(array, group, ways)
-
-    ac = fitted_ac.reshape(NA * C, Q)
-    across = sent(ac, lambda e, z, y: (e, z, y ^ 1))
-    blocks = [sent(array, lambda e, z, y: (z, e ^ m, y)) for array in (ac, across) for m in range(2)]
-
-    halves = fitted_bd.reshape(2, HALF, D * Q)
-    units = []
-    for dy in range(2):
-        half = lax.dynamic_index_in_dim(halves, yh ^ dy, 0, keepdims=False)
-        units.append(sent(half, lambda e, z, y: (z, e, y ^ dy)))
-    flat = jnp.transpose(amplitudes, (1, 2, 0)).reshape(1, D * NP)
-    peer = lax.ppermute(flat, "core", [(0, 1), (1, 0)])
-    two = jnp.where(core == 0, jnp.concatenate([flat, peer], axis=1), jnp.concatenate([peer, flat], axis=1))
-    bd = lax.all_to_all(make_unit(*units, two, across), ("yl", "x"), 0, 0, tiled=True)
-    amp = bd[:, 2 * HALF, :2 * D * NP].reshape(C, D * NP)
-
-    m = (zp ^ core).astype(jnp.int32)[None]
+    m = (zl % 2).astype(jnp.int32)[None]
     for_other = multiply(m ^ 1, amp, blocks, bd)
     for_self = multiply(m, amp, blocks, bd)
     pieces = (for_self + lax.ppermute(for_other, "core", [(0, 1), (1, 0)])).astype(jnp.bfloat16)
-    summed = finish(lax.all_to_all(pieces, "zh", 0, 0, tiled=True))
+    summed = finish(lax.all_to_all(pieces, ("zq", "yh"), 0, 0, tiled=True))
     return jnp.transpose(summed, (1, 2, 0))
 
 
 def solution(mesh):
-    fine = Mesh(mesh.devices.reshape(2, 4, 2, 8, 2, 2), ROW + COL)
+    fine = Mesh(mesh.devices.reshape(2, 2, 2, 2, 4, 4, 2), ROW + COL)
     return jax.shard_map(
         on_device,
         mesh=fine,

time: 101 us -> 93.9 us (0.930)
  the two profiles are of different devices: /device:TPU:1 before, /device:TPU:66 now
where the time goes in v4:
time: 93.9 us; the launch traced here: 93.5 us
  blocking collectives  37.5 us (40%)
  starting transfers between devices  34.8 us (37%)
  waiting for transfers between devices  11.7 us (12%)
  Pallas kernels  8.58 us (9%)
    all_to_all x1, blocking collectives, on_device(): summed = finish(lax.all_to_all(pieces, ('zq', 'yh'), 0, 0, tiled=True))  37.5 us
    all_to_all x1, starting transfers between devices, on_device(): lax.all_to_all(make_unit(core.astype(jnp.int32)[None], shard, amp, peer),...  11.9 us
    ppermute x4, starting transfers between devices, on_device(): blocks[h, m] = lax.ppermute(ac, ('core', 'zq', 'zl'), ways)  11.1 us
    all_to_all x1, waiting for transfers between devices, on_device(): lax.all_to_all(make_unit(core.astype(jnp.int32)[None], shard, amp, peer),...  6.57 us
    pallas_call x2, Pallas kernels, multiply(): pl.pallas_call(product_kernel, in_specs=[pl.BlockSpec(memory_space=pltpu....  6.26 us
    ppermute x1, starting transfers between devices, on_device(): lax.ppermute(for_other, 'core', [(0, 1), (1, 0)])  5.9 us
    ppermute x1, starting transfers between devices, on_device(): peer = lax.ppermute(amp, 'core', [(0, 1), (1, 0)])  4.27 us
    ppermute x4, waiting for transfers between devices, on_device(): blocks[h, m] = lax.ppermute(ac, ('core', 'zq', 'zl'), ways)  4.12 us
  transfers between devices with their start and end apart: 8, of which 3 were waited for; matrix products, arithmetic and copies ran while one was open for 0% of the time, Pallas kernels for 3%

profile of v4, /device:TPU:66, one launch (start us, length us, event | category | flops | bytes accessed | tf_op | source)
XLA Modules:
  0.0 93.5 jit_solution(3846863995966088265)
XLA Ops:
  0.0 1.6 %collective-permute-start = (bf16[100,8,128]{2,1,0:T(8,128)(2,1)}, bf16[100,8,128]{2,1,0:T(8,128)(2,1)S(1)}, u32[]{:S(2)}, u32[]{:S(2)}) collective-permute-start(bf16[100,8,128]{2,1,0:T(8,128)(2,1)} %param.4), channel_id=1, source_target_pairs={{0,64},{2,32},{4,0},{6,104},{8,72},{10,40},{12,8},{14,112},{16,80}... | collective-permute-start | bytes 614408 | tf_op jit(solution)/shard_map/ppermute | solution.py:169
  1.6 4.3 %collective-permute-start.1 = (bf16[4,8]{1,0:T(4,128)(2,1)}, bf16[4,8]{1,0:T(4,128)(2,1)S(1)}, u32[]{:S(2)}, u32[]{:S(2)}) collective-permute-start(bf16[4,8]{1,0:T(4,128)(2,1)} %bitcast.5), channel_id=1, source_target_pairs={{0,32},{32,0},{1,33},{33,1},{2,34},{34,2},{3,35},{35,3},{4,36},{36... | collective-permute-start | bytes 200 | tf_op jit(solution)/shard_map/ppermute | solution.py:171
  5.9 1.0 %collective-permute-done.1.peer_ref = bf16[4,8]{1,0:T(4,128)(2,1)S(1)} collective-permute-done((bf16[4,8]{1,0:T(4,128)(2,1)}, bf16[4,8]{1,0:T(4,128)(2,1)S(1)}, u32[]{:S(2)}, u32[]{:S(2)}) %collective-permute-start.1) | collective-permute-done | bytes 96 | tf_op jit(solution)/shard_map/ppermute | solution.py:171
  6.9 0.0 collective-permute-done.bd_ref
  6.9 0.0 copy-start
  6.9 0.7 copy-done
  7.5 1.5 %make_unit.1 = bf16[8,104,1024]{2,1,0:T(8,128)(2,1)} custom-call(s32[1]{0:T(128)} %bitcast.1.core_ref, bf16[100,8,128]{2,1,0:T(8,128)(2,1)S(1)} %collective-permute-done.bd_ref, bf16[4,8]{1,0:T(4,128)(2,1)S(1)} %bitcast.6, bf16[4,8]{1,0:T(4,128)(2,1)S(1)} %collective-permute-done.1.peer_ref), custom_call_target="tpu_custom_call" | custom-call | tf_op jit(solution)/shard_map/make_unit/pallas_call | solution.py:66
  9.0 11.9 %all-to-all-start = ((bf16[8,104,1024]{2,1,0:T(8,128)(2,1)}), bf16[8,104,1024]{2,1,0:T(8,128)(2,1)S(1)}, u32[]{:S(2)}, u32[]{:S(2)}) async-start(bf16[8,104,1024]{2,1,0:T(8,128)(2,1)} %make_unit.1), calls=%async_computation | async-start | bytes 3407872 | tf_op jit(solution)/shard_map/all_to_all | solution.py:172
  21.0 5.2 %collective-permute-start.2 = (bf16[1600,128]{1,0:T(8,128)(2,1)}, bf16[1600,128]{1,0:T(8,128)(2,1)S(1)}, u32[]{:S(2)}, u32[]{:S(2)}) collective-permute-start(bf16[1600,128]{1,0:T(8,128)(2,1)} %bitcast.3), channel_id=1, source_target_pairs={{0,28},{2,38},{4,0},{6,42},{8,4},{10,46},{12,8},{14,50},{16,12},{1... | collective-permute-start | bytes 1228808 | tf_op jit(solution)/shard_map/ppermute | solution.py:178
  26.2 1.9 %collective-permute-start.3 = (bf16[1600,128]{1,0:T(8,128)(2,1)}, bf16[1600,128]{1,0:T(8,128)(2,1)S(1)}, u32[]{:S(2)}, u32[]{:S(2)}) collective-permute-start(bf16[1600,128]{1,0:T(8,128)(2,1)} %bitcast.3), channel_id=1, source_target_pairs={{0,30},{2,32},{4,2},{6,36},{8,6},{10,40},{12,10},{14,44},{16,14},{... | collective-permute-start | bytes 1228808 | tf_op jit(solution)/shard_map/ppermute | solution.py:178
  28.1 1.7 %collective-permute-start.4 = (bf16[1600,128]{1,0:T(8,128)(2,1)}, bf16[1600,128]{1,0:T(8,128)(2,1)S(1)}, u32[]{:S(2)}, u32[]{:S(2)}) collective-permute-start(bf16[1600,128]{1,0:T(8,128)(2,1)} %bitcast.3), channel_id=1, source_target_pairs={{0,0},{2,34},{4,4},{6,38},{8,8},{10,42},{12,12},{14,46},{16,16},{1... | collective-permute-start | bytes 1228808 | tf_op jit(solution)/shard_map/ppermute | solution.py:178
  29.8 2.3 %collective-permute-start.5 = (bf16[1600,128]{1,0:T(8,128)(2,1)}, bf16[1600,128]{1,0:T(8,128)(2,1)S(1)}, u32[]{:S(2)}, u32[]{:S(2)}) collective-permute-start(bf16[1600,128]{1,0:T(8,128)(2,1)} %bitcast.3), channel_id=1, source_target_pairs={{0,2},{2,36},{4,6},{6,40},{8,10},{10,44},{12,14},{14,48},{16,18},{... | collective-permute-start | bytes 1228808 | tf_op jit(solution)/shard_map/ppermute | solution.py:178
  32.1 6.6 %all-to-all-done.bd_ref = bf16[8,104,1024]{2,1,0:T(8,128)(2,1)S(1)} async-done(((bf16[8,104,1024]{2,1,0:T(8,128)(2,1)}), bf16[8,104,1024]{2,1,0:T(8,128)(2,1)S(1)}, u32[]{:S(2)}, u32[]{:S(2)}) %all-to-all-start) | async-done | bytes 1703968 | tf_op jit(solution)/shard_map/all_to_all | solution.py:172
  38.7 0.1 reshape_squeeze.3.amp_ref
  38.8 0.0 collective-permute-done.2.ac00_ref
  38.8 4.1 %collective-permute-done.3.ac01_ref = bf16[1600,128]{1,0:T(8,128)(2,1)S(1)} collective-permute-done((bf16[1600,128]{1,0:T(8,128)(2,1)}, bf16[1600,128]{1,0:T(8,128)(2,1)S(1)}, u32[]{:S(2)}, u32[]{:S(2)}) %collective-permute-start.3) | collective-permute-done | bytes 409632 | tf_op jit(solution)/shard_map/ppermute | solution.py:178
  42.9 0.0 collective-permute-done.4.ac10_ref
  42.9 0.0 collective-permute-done.5.ac11_ref
  42.9 3.1 %multiply.3 = f32[8,160,128]{2,1,0:T(8,128)S(1)} custom-call(s32[1]{0:T(128)S(6)} %xor.3.m_ref, bf16[16,32]{1,0:T(8,128)(2,1)S(1)} %reshape_squeeze.3.amp_ref, bf16[1600,128]{1,0:T(8,128)(2,1)S(1)} %collective-permute-done.2.ac00_ref, bf16[1600,128]{1,0:T(8,128)(2,1)S(1)} %collective-permute-done.3.ac01_ref, ...), custom_call_target="tpu_custom_call" | custom-call | flops 1310720000 | bytes 6291456 | tf_op jit(solution)/shard_map/multiply/pallas_call | solution.py:120
  46.0 5.9 %collective-permute-start.6 = (f32[8,160,128]{2,1,0:T(8,128)S(1)}, f32[8,160,128]{2,1,0:T(8,128)S(1)}, u32[]{:S(2)}, u32[]{:S(2)}) collective-permute-start(f32[8,160,128]{2,1,0:T(8,128)S(1)} %multiply.3), channel_id=1, source_target_pairs={{0,32},{32,0},{1,33},{33,1},{2,34},{34,2},{3,35},{35,3},{4,36},{36... | collective-permute-start | bytes 1966088 | tf_op jit(solution)/shard_map/ppermute | solution.py:185
  52.0 3.1 %multiply.2 = f32[8,160,128]{2,1,0:T(8,128)S(1)} custom-call(s32[1]{0:T(128)} %bitcast.m_ref, bf16[16,32]{1,0:T(8,128)(2,1)S(1)} %reshape_squeeze.3.amp_ref, bf16[1600,128]{1,0:T(8,128)(2,1)S(1)} %collective-permute-done.2.ac00_ref, bf16[1600,128]{1,0:T(8,128)(2,1)S(1)} %collective-permute-done.3.ac01_ref, ...), custom_call_target="tpu_custom_call" | custom-call | flops 1310720000 | bytes 6291456 | tf_op jit(solution)/shard_map/multiply/pallas_call | solution.py:120
  55.1 0.0 collective-permute-done.6
  55.1 0.1 add_convert_fusion
  55.2 37.5 %all_to_all.10.parts_ref = bf16[8,160,128]{2,1,0:T(8,128)(2,1)S(1)} all-to-all(bf16[8,160,128]{2,1,0:T(8,128)(2,1)S(1)} %add_convert_fusion), channel_id=1, replica_groups=mesh['yl'=2,'xh'=2,'xl'=2,'core'=2,'zq'=4,'zl'=4,'yh'=2] {'zq','yh'}, dimensions={0} | all-to-all | bytes 655360 | tf_op jit(solution)/shard_map/all_to_all | solution.py:186
  92.7 0.8 finish.1
  (1 shorter events, 0.0 us)
Async XLA Ops:
  0.0 6.9 %collective-permute-start = (bf16[100,8,128]{2,1,0:T(8,128)(2,1)}, bf16[100,8,128]{2,1,0:T(8,128)(2,1)S(1)}, u32[]{:S(2)}, u32[]{:S(2)}) collective-permute-start(bf16[100,8,128]{2,1,0:T(8,128)(2,1)} %param.4), channel_id=1, source_target_pairs={{0,64},{2,32},{4,0},{6,104},{8,72},{10,40},{12,8},{14,112},{16,80}... | collective-permute-start | bytes 614408 | tf_op jit(solution)/shard_map/ppermute | solution.py:169
  1.6 5.3 %collective-permute-start.1 = (bf16[4,8]{1,0:T(4,128)(2,1)}, bf16[4,8]{1,0:T(4,128)(2,1)S(1)}, u32[]{:S(2)}, u32[]{:S(2)}) collective-permute-start(bf16[4,8]{1,0:T(4,128)(2,1)} %bitcast.5), channel_id=1, source_target_pairs={{0,32},{32,0},{1,33},{33,1},{2,34},{34,2},{3,35},{35,3},{4,36},{36... | collective-permute-start | bytes 200 | tf_op jit(solution)/shard_map/ppermute | solution.py:171
  6.9 0.7 copy-start
  9.0 29.6 %all-to-all-start = ((bf16[8,104,1024]{2,1,0:T(8,128)(2,1)}), bf16[8,104,1024]{2,1,0:T(8,128)(2,1)S(1)}, u32[]{:S(2)}, u32[]{:S(2)}) async-start(bf16[8,104,1024]{2,1,0:T(8,128)(2,1)} %make_unit.1), calls=%async_computation | async-start | bytes 3407872 | tf_op jit(solution)/shard_map/all_to_all | solution.py:172
  21.0 17.8 %collective-permute-start.2 = (bf16[1600,128]{1,0:T(8,128)(2,1)}, bf16[1600,128]{1,0:T(8,128)(2,1)S(1)}, u32[]{:S(2)}, u32[]{:S(2)}) collective-permute-start(bf16[1600,128]{1,0:T(8,128)(2,1)} %bitcast.3), channel_id=1, source_target_pairs={{0,28},{2,38},{4,0},{6,42},{8,4},{10,46},{12,8},{14,50},{16,12},{1... | collective-permute-start | bytes 1228808 | tf_op jit(solution)/shard_map/ppermute | solution.py:178
  26.2 16.7 %collective-permute-start.3 = (bf16[1600,128]{1,0:T(8,128)(2,1)}, bf16[1600,128]{1,0:T(8,128)(2,1)S(1)}, u32[]{:S(2)}, u32[]{:S(2)}) collective-permute-start(bf16[1600,128]{1,0:T(8,128)(2,1)} %bitcast.3), channel_id=1, source_target_pairs={{0,30},{2,32},{4,2},{6,36},{8,6},{10,40},{12,10},{14,44},{16,14},{... | collective-permute-start | bytes 1228808 | tf_op jit(solution)/shard_map/ppermute | solution.py:178
  28.1 14.8 %collective-permute-start.4 = (bf16[1600,128]{1,0:T(8,128)(2,1)}, bf16[1600,128]{1,0:T(8,128)(2,1)S(1)}, u32[]{:S(2)}, u32[]{:S(2)}) collective-permute-start(bf16[1600,128]{1,0:T(8,128)(2,1)} %bitcast.3), channel_id=1, source_target_pairs={{0,0},{2,34},{4,4},{6,38},{8,8},{10,42},{12,12},{14,46},{16,16},{1... | collective-permute-start | bytes 1228808 | tf_op jit(solution)/shard_map/ppermute | solution.py:178
  29.8 13.1 %collective-permute-start.5 = (bf16[1600,128]{1,0:T(8,128)(2,1)}, bf16[1600,128]{1,0:T(8,128)(2,1)S(1)}, u32[]{:S(2)}, u32[]{:S(2)}) collective-permute-start(bf16[1600,128]{1,0:T(8,128)(2,1)} %bitcast.3), channel_id=1, source_target_pairs={{0,2},{2,36},{4,6},{6,40},{8,10},{10,44},{12,14},{14,48},{16,18},{... | collective-permute-start | bytes 1228808 | tf_op jit(solution)/shard_map/ppermute | solution.py:178
  46.0 9.0 %collective-permute-start.6 = (f32[8,160,128]{2,1,0:T(8,128)S(1)}, f32[8,160,128]{2,1,0:T(8,128)S(1)}, u32[]{:S(2)}, u32[]{:S(2)}) collective-permute-start(f32[8,160,128]{2,1,0:T(8,128)S(1)} %multiply.3), channel_id=1, source_target_pairs={{0,32},{32,0},{1,33},{33,1},{2,34},{34,2},{3,35},{35,3},{4,36},{36... | collective-permute-start | bytes 1966088 | tf_op jit(solution)/shard_map/ppermute | solution.py:185

commit v5 on v4

--- a/solution.py
+++ b/solution.py
@@ -50,7 +50,7 @@
     for d in range(D):
         unit_ref[0:NB, d * Q:(d + 1) * Q] = wide_ref[pl.ds(d, NB, stride=D), :].astype(jnp.bfloat16)
     unit_ref[NB:, :] = jnp.zeros((UNIT - NB, D * Q), jnp.bfloat16)
-    own, peer = in_a_row(amp_ref[...]), in_a_row(peer_ref[...])
+    own, peer = in_a_row(amp_ref[...].astype(jnp.bfloat16)), in_a_row(peer_ref[...])
     first = core_ref[0] == 0
     both = jnp.concatenate([jnp.where(first, own, peer), jnp.where(first, peer, own)], axis=1)
     unit_ref[NB:NB + 1, 0:2 * D * NP] = both.astype(jnp.bfloat16)
@@ -169,7 +169,7 @@
     shard = lax.ppermute(fitted_bd, ("xl", "core", "zq", "zl"), ways)
     amp = amplitudes.reshape(NP, D)
     peer = lax.ppermute(amp, "core", [(0, 1), (1, 0)])
-    bd = lax.all_to_all(make_unit(core.astype(jnp.int32)[None], shard, amp, peer), ("yl", "xh", "xl"), 0, 0, tiled=True)
+    bd = lax.all_to_all(make_unit(core.astype(jnp.int32)[None], shard, amp.astype(jnp.float32), peer), ("yl", "xh", "xl"), 0, 0, tiled=True)
     ac = fitted_ac.reshape(NA * C, Q)
     blocks = {}
     for h in range(2):

time: 93.9 us -> 93.2 us (level)
  transfers between devices with their start and end apart: 8 -> 8, of which waited for: 3 -> 3; matrix products, arithmetic and copies ran while one was open for 0% -> 1% of each run, Pallas kernels for 3% -> 3%
where the time goes in v5:
time: 93.2 us; the launch traced here: 92.8 us
  blocking collectives  37.5 us (40%)
  starting transfers between devices  34.8 us (37%)
  waiting for transfers between devices  11 us (12%)
  Pallas kernels  8.58 us (9%)
    all_to_all x1, blocking collectives, on_device(): summed = finish(lax.all_to_all(pieces, ('zq', 'yh'), 0, 0, tiled=True))  37.5 us
    all_to_all x1, starting transfers between devices, on_device(): lax.all_to_all(make_unit(core.astype(jnp.int32)[None], shard, amp.astype(...  11.9 us
    ppermute x4, starting transfers between devices, on_device(): blocks[h, m] = lax.ppermute(ac, ('core', 'zq', 'zl'), ways)  11.1 us
    all_to_all x1, waiting for transfers between devices, on_device(): lax.all_to_all(make_unit(core.astype(jnp.int32)[None], shard, amp.astype(...  6.57 us
    pallas_call x2, Pallas kernels, multiply(): pl.pallas_call(product_kernel, in_specs=[pl.BlockSpec(memory_space=pltpu....  6.26 us
    ppermute x1, starting transfers between devices, on_device(): lax.ppermute(for_other, 'core', [(0, 1), (1, 0)])  5.9 us
    ppermute x1, starting transfers between devices, on_device(): peer = lax.ppermute(amp, 'core', [(0, 1), (1, 0)])  4.27 us
    ppermute x4, waiting for transfers between devices, on_device(): blocks[h, m] = lax.ppermute(ac, ('core', 'zq', 'zl'), ways)  4.12 us
  transfers between devices with their start and end apart: 8, of which 3 were waited for; matrix products, arithmetic and copies ran while one was open for 1% of the time, Pallas kernels for 3%

profile of v5, /device:TPU:66, one launch (start us, length us, event | category | flops | bytes accessed | tf_op | source)
XLA Modules:
  0.0 92.8 jit_solution(3037344309195541957)
XLA Ops:
  0.0 1.6 %collective-permute-start = (bf16[100,8,128]{2,1,0:T(8,128)(2,1)}, bf16[100,8,128]{2,1,0:T(8,128)(2,1)S(1)}, u32[]{:S(2)}, u32[]{:S(2)}) collective-permute-start(bf16[100,8,128]{2,1,0:T(8,128)(2,1)} %param.4), channel_id=1, source_target_pairs={{0,64},{2,32},{4,0},{6,104},{8,72},{10,40},{12,8},{14,112},{16,80}... | collective-permute-start | bytes 614408 | tf_op jit(solution)/shard_map/ppermute | solution.py:169
  1.6 4.3 %collective-permute-start.1 = (bf16[4,8]{1,0:T(4,128)(2,1)}, bf16[4,8]{1,0:T(4,128)(2,1)S(1)}, u32[]{:S(2)}, u32[]{:S(2)}) collective-permute-start(bf16[4,8]{1,0:T(4,128)(2,1)} %bitcast.6), channel_id=1, source_target_pairs={{0,32},{32,0},{1,33},{33,1},{2,34},{34,2},{3,35},{35,3},{4,36},{36... | collective-permute-start | bytes 200 | tf_op jit(solution)/shard_map/ppermute | solution.py:171
  5.9 0.7 bitcast_convert_fusion.amp_ref
  6.5 0.3 collective-permute-done.1.peer_ref
  6.9 0.0 collective-permute-done.bd_ref
  6.9 1.5 %make_unit.1 = bf16[8,104,1024]{2,1,0:T(8,128)(2,1)} custom-call(s32[1]{0:T(128)} %bitcast.1.core_ref, bf16[100,8,128]{2,1,0:T(8,128)(2,1)S(1)} %collective-permute-done.bd_ref, f32[4,8]{1,0:T(4,128)S(1)} %bitcast_convert_fusion.amp_ref, bf16[4,8]{1,0:T(4,128)(2,1)S(1)} %collective-permute-done.1.peer_ref), custom_call_target="tpu_custom_call" | custom-call | tf_op jit(solution)/shard_map/make_unit/pallas_call | solution.py:66
  8.4 11.9 %all-to-all-start = ((bf16[8,104,1024]{2,1,0:T(8,128)(2,1)}), bf16[8,104,1024]{2,1,0:T(8,128)(2,1)S(1)}, u32[]{:S(2)}, u32[]{:S(2)}) async-start(bf16[8,104,1024]{2,1,0:T(8,128)(2,1)} %make_unit.1), calls=%async_computation | async-start | bytes 3407872 | tf_op jit(solution)/shard_map/all_to_all | solution.py:172
  20.3 5.2 %collective-permute-start.2 = (bf16[1600,128]{1,0:T(8,128)(2,1)}, bf16[1600,128]{1,0:T(8,128)(2,1)S(1)}, u32[]{:S(2)}, u32[]{:S(2)}) collective-permute-start(bf16[1600,128]{1,0:T(8,128)(2,1)} %bitcast.3), channel_id=1, source_target_pairs={{0,28},{2,38},{4,0},{6,42},{8,4},{10,46},{12,8},{14,50},{16,12},{1... | collective-permute-start | bytes 1228808 | tf_op jit(solution)/shard_map/ppermute | solution.py:178
  25.5 1.9 %collective-permute-start.3 = (bf16[1600,128]{1,0:T(8,128)(2,1)}, bf16[1600,128]{1,0:T(8,128)(2,1)S(1)}, u32[]{:S(2)}, u32[]{:S(2)}) collective-permute-start(bf16[1600,128]{1,0:T(8,128)(2,1)} %bitcast.3), channel_id=1, source_target_pairs={{0,30},{2,32},{4,2},{6,36},{8,6},{10,40},{12,10},{14,44},{16,14},{... | collective-permute-start | bytes 1228808 | tf_op jit(solution)/shard_map/ppermute | solution.py:178
  27.4 1.7 %collective-permute-start.4 = (bf16[1600,128]{1,0:T(8,128)(2,1)}, bf16[1600,128]{1,0:T(8,128)(2,1)S(1)}, u32[]{:S(2)}, u32[]{:S(2)}) collective-permute-start(bf16[1600,128]{1,0:T(8,128)(2,1)} %bitcast.3), channel_id=1, source_target_pairs={{0,0},{2,34},{4,4},{6,38},{8,8},{10,42},{12,12},{14,46},{16,16},{1... | collective-permute-start | bytes 1228808 | tf_op jit(solution)/shard_map/ppermute | solution.py:178
  29.1 2.3 %collective-permute-start.5 = (bf16[1600,128]{1,0:T(8,128)(2,1)}, bf16[1600,128]{1,0:T(8,128)(2,1)S(1)}, u32[]{:S(2)}, u32[]{:S(2)}) collective-permute-start(bf16[1600,128]{1,0:T(8,128)(2,1)} %bitcast.3), channel_id=1, source_target_pairs={{0,2},{2,36},{4,6},{6,40},{8,10},{10,44},{12,14},{14,48},{16,18},{... | collective-permute-start | bytes 1228808 | tf_op jit(solution)/shard_map/ppermute | solution.py:178
  31.4 6.6 %all-to-all-done.bd_ref = bf16[8,104,1024]{2,1,0:T(8,128)(2,1)S(1)} async-done(((bf16[8,104,1024]{2,1,0:T(8,128)(2,1)}), bf16[8,104,1024]{2,1,0:T(8,128)(2,1)S(1)}, u32[]{:S(2)}, u32[]{:S(2)}) %all-to-all-start) | async-done | bytes 1703968 | tf_op jit(solution)/shard_map/all_to_all | solution.py:172
  38.0 0.1 reshape_squeeze.3.amp_ref
  38.1 0.0 collective-permute-done.2.ac00_ref
  38.1 4.1 %collective-permute-done.3.ac01_ref = bf16[1600,128]{1,0:T(8,128)(2,1)S(1)} collective-permute-done((bf16[1600,128]{1,0:T(8,128)(2,1)}, bf16[1600,128]{1,0:T(8,128)(2,1)S(1)}, u32[]{:S(2)}, u32[]{:S(2)}) %collective-permute-start.3) | collective-permute-done | bytes 409632 | tf_op jit(solution)/shard_map/ppermute | solution.py:178
  42.2 0.0 collective-permute-done.4.ac10_ref
  42.2 0.0 collective-permute-done.5.ac11_ref
  42.2 3.1 %multiply.3 = f32[8,160,128]{2,1,0:T(8,128)S(1)} custom-call(s32[1]{0:T(128)S(6)} %xor.3.m_ref, bf16[16,32]{1,0:T(8,128)(2,1)S(1)} %reshape_squeeze.3.amp_ref, bf16[1600,128]{1,0:T(8,128)(2,1)S(1)} %collective-permute-done.2.ac00_ref, bf16[1600,128]{1,0:T(8,128)(2,1)S(1)} %collective-permute-done.3.ac01_ref, ...), custom_call_target="tpu_custom_call" | custom-call | flops 1310720000 | bytes 6291456 | tf_op jit(solution)/shard_map/multiply/pallas_call | solution.py:120
  45.4 5.9 %collective-permute-start.6 = (f32[8,160,128]{2,1,0:T(8,128)S(1)}, f32[8,160,128]{2,1,0:T(8,128)S(1)}, u32[]{:S(2)}, u32[]{:S(2)}) collective-permute-start(f32[8,160,128]{2,1,0:T(8,128)S(1)} %multiply.3), channel_id=1, source_target_pairs={{0,32},{32,0},{1,33},{33,1},{2,34},{34,2},{3,35},{35,3},{4,36},{36... | collective-permute-start | bytes 1966088 | tf_op jit(solution)/shard_map/ppermute | solution.py:185
  51.3 3.1 %multiply.2 = f32[8,160,128]{2,1,0:T(8,128)S(1)} custom-call(s32[1]{0:T(128)} %bitcast.m_ref, bf16[16,32]{1,0:T(8,128)(2,1)S(1)} %reshape_squeeze.3.amp_ref, bf16[1600,128]{1,0:T(8,128)(2,1)S(1)} %collective-permute-done.2.ac00_ref, bf16[1600,128]{1,0:T(8,128)(2,1)S(1)} %collective-permute-done.3.ac01_ref, ...), custom_call_target="tpu_custom_call" | custom-call | flops 1310720000 | bytes 6291456 | tf_op jit(solution)/shard_map/multiply/pallas_call | solution.py:120
  54.4 0.0 collective-permute-done.6
  54.4 0.1 add_convert_fusion
  54.5 37.5 %all_to_all.10.parts_ref = bf16[8,160,128]{2,1,0:T(8,128)(2,1)S(1)} all-to-all(bf16[8,160,128]{2,1,0:T(8,128)(2,1)S(1)} %add_convert_fusion), channel_id=1, replica_groups=mesh['yl'=2,'xh'=2,'xl'=2,'core'=2,'zq'=4,'zl'=4,'yh'=2] {'zq','yh'}, dimensions={0} | all-to-all | bytes 655360 | tf_op jit(solution)/shard_map/all_to_all | solution.py:186
  92.0 0.8 finish.1
  (1 shorter events, 0.0 us)
Async XLA Ops:
  0.0 6.9 %collective-permute-start = (bf16[100,8,128]{2,1,0:T(8,128)(2,1)}, bf16[100,8,128]{2,1,0:T(8,128)(2,1)S(1)}, u32[]{:S(2)}, u32[]{:S(2)}) collective-permute-start(bf16[100,8,128]{2,1,0:T(8,128)(2,1)} %param.4), channel_id=1, source_target_pairs={{0,64},{2,32},{4,0},{6,104},{8,72},{10,40},{12,8},{14,112},{16,80}... | collective-permute-start | bytes 614408 | tf_op jit(solution)/shard_map/ppermute | solution.py:169
  1.6 5.3 %collective-permute-start.1 = (bf16[4,8]{1,0:T(4,128)(2,1)}, bf16[4,8]{1,0:T(4,128)(2,1)S(1)}, u32[]{:S(2)}, u32[]{:S(2)}) collective-permute-start(bf16[4,8]{1,0:T(4,128)(2,1)} %bitcast.6), channel_id=1, source_target_pairs={{0,32},{32,0},{1,33},{33,1},{2,34},{34,2},{3,35},{35,3},{4,36},{36... | collective-permute-start | bytes 200 | tf_op jit(solution)/shard_map/ppermute | solution.py:171
  8.4 29.6 %all-to-all-start = ((bf16[8,104,1024]{2,1,0:T(8,128)(2,1)}), bf16[8,104,1024]{2,1,0:T(8,128)(2,1)S(1)}, u32[]{:S(2)}, u32[]{:S(2)}) async-start(bf16[8,104,1024]{2,1,0:T(8,128)(2,1)} %make_unit.1), calls=%async_computation | async-start | bytes 3407872 | tf_op jit(solution)/shard_map/all_to_all | solution.py:172
  20.3 17.8 %collective-permute-start.2 = (bf16[1600,128]{1,0:T(8,128)(2,1)}, bf16[1600,128]{1,0:T(8,128)(2,1)S(1)}, u32[]{:S(2)}, u32[]{:S(2)}) collective-permute-start(bf16[1600,128]{1,0:T(8,128)(2,1)} %bitcast.3), channel_id=1, source_target_pairs={{0,28},{2,38},{4,0},{6,42},{8,4},{10,46},{12,8},{14,50},{16,12},{1... | collective-permute-start | bytes 1228808 | tf_op jit(solution)/shard_map/ppermute | solution.py:178
  25.5 16.7 %collective-permute-start.3 = (bf16[1600,128]{1,0:T(8,128)(2,1)}, bf16[1600,128]{1,0:T(8,128)(2,1)S(1)}, u32[]{:S(2)}, u32[]{:S(2)}) collective-permute-start(bf16[1600,128]{1,0:T(8,128)(2,1)} %bitcast.3), channel_id=1, source_target_pairs={{0,30},{2,32},{4,2},{6,36},{8,6},{10,40},{12,10},{14,44},{16,14},{... | collective-permute-start | bytes 1228808 | tf_op jit(solution)/shard_map/ppermute | solution.py:178
  27.4 14.8 %collective-permute-start.4 = (bf16[1600,128]{1,0:T(8,128)(2,1)}, bf16[1600,128]{1,0:T(8,128)(2,1)S(1)}, u32[]{:S(2)}, u32[]{:S(2)}) collective-permute-start(bf16[1600,128]{1,0:T(8,128)(2,1)} %bitcast.3), channel_id=1, source_target_pairs={{0,0},{2,34},{4,4},{6,38},{8,8},{10,42},{12,12},{14,46},{16,16},{1... | collective-permute-start | bytes 1228808 | tf_op jit(solution)/shard_map/ppermute | solution.py:178
  29.1 13.1 %collective-permute-start.5 = (bf16[1600,128]{1,0:T(8,128)(2,1)}, bf16[1600,128]{1,0:T(8,128)(2,1)S(1)}, u32[]{:S(2)}, u32[]{:S(2)}) collective-permute-start(bf16[1600,128]{1,0:T(8,128)(2,1)} %bitcast.3), channel_id=1, source_target_pairs={{0,2},{2,36},{4,6},{6,40},{8,10},{10,44},{12,14},{14,48},{16,18},{... | collective-permute-start | bytes 1228808 | tf_op jit(solution)/shard_map/ppermute | solution.py:178
  45.4 9.1 %collective-permute-start.6 = (f32[8,160,128]{2,1,0:T(8,128)S(1)}, f32[8,160,128]{2,1,0:T(8,128)S(1)}, u32[]{:S(2)}, u32[]{:S(2)}) collective-permute-start(f32[8,160,128]{2,1,0:T(8,128)S(1)} %multiply.3), channel_id=1, source_target_pairs={{0,32},{32,0},{1,33},{33,1},{2,34},{34,2},{3,35},{35,3},{4,36},{36... | collective-permute-start | bytes 1966088 | tf_op jit(solution)/shard_map/ppermute | solution.py:185

commit v6 on v5

--- a/solution.py
+++ b/solution.py
@@ -7,6 +7,7 @@
 
 ROW = ("yl", "xh", "xl", "core")
 COL = ("zq", "zl", "yh")
+ORDER = (2, 3, 0, 1)
 DELTA = ((2, 1), (0, 3))
 HALF_OF = (1, 0, 0, 1)
 NT = (((1,), (1,)), ((), ()))
@@ -107,13 +108,14 @@
     )
     for t in range(8):
         at = slice(HALF * t, HALF * (t + 1))
+        to = 2 * ORDER.index(t // 2) + t % 2
         last = acc_ref[at, 3 * WIDE:3 * WIDE + NA]
         for j in range(3):
-            out_ref[t, 50 * j:50 * j + 50, :] = jnp.concatenate(
+            out_ref[to, 50 * j:50 * j + 50, :] = jnp.concatenate(
                 [acc_ref[at, WIDE * j:WIDE * j + NA], last[:, 28 * j:28 * j + 28]], axis=1
             )
         rest = [last[10 * g:10 * g + 10, 84:100] for g in range(5)]
-        out_ref[t, 150:160, :] = jnp.concatenate(rest + [jnp.zeros((10, 48), jnp.float32)], axis=1)
+        out_ref[to, 150:160, :] = jnp.concatenate(rest + [jnp.zeros((10, 48), jnp.float32)], axis=1)
 
 
 def multiply(m, amp, blocks, bd):
@@ -183,7 +185,8 @@
     for_other = multiply(m ^ 1, amp, blocks, bd)
     for_self = multiply(m, amp, blocks, bd)
     pieces = (for_self + lax.ppermute(for_other, "core", [(0, 1), (1, 0)])).astype(jnp.bfloat16)
-    summed = finish(lax.all_to_all(pieces, ("zq", "yh"), 0, 0, tiled=True))
+    groups = [[8 * zq + 2 * f + y for zq in ORDER for y in range(2)] for f in range(4)]
+    summed = finish(lax.all_to_all(pieces, COL, 0, 0, axis_index_groups=groups, tiled=True))
     return jnp.transpose(summed, (1, 2, 0))
 
 

time: 93.2 us -> 89.4 us (0.959)
  the two profiles are of different devices: /device:TPU:66 before, /device:TPU:1 now
where the time goes in v6:
time: 89.4 us; the launch traced here: 89 us
  starting transfers between devices  37.3 us (42%)
  blocking collectives  30.3 us (34%)
  waiting for transfers between devices  11.7 us (13%)
  Pallas kernels  8.58 us (10%)
    all_to_all x1, blocking collectives, on_device(): lax.all_to_all(pieces, COL, 0, 0, axis_index_groups=groups, tiled=True)  30.3 us
    ppermute x4, starting transfers between devices, on_device(): blocks[h, m] = lax.ppermute(ac, ('core', 'zq', 'zl'), ways)  13.9 us
    all_to_all x1, starting transfers between devices, on_device(): lax.all_to_all(make_unit(core.astype(jnp.int32)[None], shard, amp.astype(...  10.8 us
    all_to_all x1, waiting for transfers between devices, on_device(): lax.all_to_all(make_unit(core.astype(jnp.int32)[None], shard, amp.astype(...  8.87 us
    pallas_call x2, Pallas kernels, multiply(): pl.pallas_call(product_kernel, in_specs=[pl.BlockSpec(memory_space=pltpu....  6.25 us
    ppermute x1, starting transfers between devices, on_device(): shard = lax.ppermute(fitted_bd, ('xl', 'core', 'zq', 'zl'), ways)  5.85 us
    ppermute x1, starting transfers between devices, on_device(): peer = lax.ppermute(amp, 'core', [(0, 1), (1, 0)])  4.84 us
    ppermute x4, waiting for transfers between devices, on_device(): blocks[h, m] = lax.ppermute(ac, ('core', 'zq', 'zl'), ways)  2.53 us
  transfers between devices with their start and end apart: 8, of which 4 were waited for; matrix products, arithmetic and copies ran while one was open for 1% of the time, Pallas kernels for 4%

profile of v6, /device:TPU:1, one launch (start us, length us, event | category | flops | bytes accessed | tf_op | source)
XLA Modules:
  0.0 89.0 jit_solution(10593161996442627996)
XLA Ops:
  0.0 5.9 %collective-permute-start = (bf16[100,8,128]{2,1,0:T(8,128)(2,1)}, bf16[100,8,128]{2,1,0:T(8,128)(2,1)S(1)}, u32[]{:S(2)}, u32[]{:S(2)}) collective-permute-start(bf16[100,8,128]{2,1,0:T(8,128)(2,1)} %param.4), channel_id=1, source_target_pairs={{0,64},{2,32},{4,0},{6,104},{8,72},{10,40},{12,8},{14,112},{16,80}... | collective-permute-start | bytes 614408 | tf_op jit(solution)/shard_map/ppermute | solution.py:171
  5.9 4.8 %collective-permute-start.1 = (bf16[4,8]{1,0:T(4,128)(2,1)}, bf16[4,8]{1,0:T(4,128)(2,1)S(1)}, u32[]{:S(2)}, u32[]{:S(2)}) collective-permute-start(bf16[4,8]{1,0:T(4,128)(2,1)} %bitcast.6), channel_id=1, source_target_pairs={{0,32},{32,0},{1,33},{33,1},{2,34},{34,2},{3,35},{35,3},{4,36},{36... | collective-permute-start | bytes 200 | tf_op jit(solution)/shard_map/ppermute | solution.py:173
  10.7 0.7 bitcast_convert_fusion.amp_ref
  11.4 0.3 collective-permute-done.1.peer_ref
  11.7 0.0 collective-permute-done.bd_ref
  11.7 1.5 %make_unit.1 = bf16[8,104,1024]{2,1,0:T(8,128)(2,1)} custom-call(s32[1]{0:T(128)} %bitcast.1.core_ref, bf16[100,8,128]{2,1,0:T(8,128)(2,1)S(1)} %collective-permute-done.bd_ref, f32[4,8]{1,0:T(4,128)S(1)} %bitcast_convert_fusion.amp_ref, bf16[4,8]{1,0:T(4,128)(2,1)S(1)} %collective-permute-done.1.peer_ref), custom_call_target="tpu_custom_call" | custom-call | tf_op jit(solution)/shard_map/make_unit/pallas_call | solution.py:67
  13.2 10.8 %all-to-all-start = ((bf16[8,104,1024]{2,1,0:T(8,128)(2,1)}), bf16[8,104,1024]{2,1,0:T(8,128)(2,1)S(1)}, u32[]{:S(2)}, u32[]{:S(2)}) async-start(bf16[8,104,1024]{2,1,0:T(8,128)(2,1)} %make_unit.1), calls=%async_computation | async-start | bytes 3407872 | tf_op jit(solution)/shard_map/all_to_all | solution.py:174
  24.0 6.4 %collective-permute-start.2 = (bf16[1600,128]{1,0:T(8,128)(2,1)}, bf16[1600,128]{1,0:T(8,128)(2,1)S(1)}, u32[]{:S(2)}, u32[]{:S(2)}) collective-permute-start(bf16[1600,128]{1,0:T(8,128)(2,1)} %bitcast.3), channel_id=1, source_target_pairs={{0,28},{2,38},{4,0},{6,42},{8,4},{10,46},{12,8},{14,50},{16,12},{1... | collective-permute-start | bytes 1228808 | tf_op jit(solution)/shard_map/ppermute | solution.py:180
  30.5 3.3 %collective-permute-start.3 = (bf16[1600,128]{1,0:T(8,128)(2,1)}, bf16[1600,128]{1,0:T(8,128)(2,1)S(1)}, u32[]{:S(2)}, u32[]{:S(2)}) collective-permute-start(bf16[1600,128]{1,0:T(8,128)(2,1)} %bitcast.3), channel_id=1, source_target_pairs={{0,30},{2,32},{4,2},{6,36},{8,6},{10,40},{12,10},{14,44},{16,14},{... | collective-permute-start | bytes 1228808 | tf_op jit(solution)/shard_map/ppermute | solution.py:180
  33.8 2.3 %collective-permute-start.4 = (bf16[1600,128]{1,0:T(8,128)(2,1)}, bf16[1600,128]{1,0:T(8,128)(2,1)S(1)}, u32[]{:S(2)}, u32[]{:S(2)}) collective-permute-start(bf16[1600,128]{1,0:T(8,128)(2,1)} %bitcast.3), channel_id=1, source_target_pairs={{0,0},{2,34},{4,4},{6,38},{8,8},{10,42},{12,12},{14,46},{16,16},{1... | collective-permute-start | bytes 1228808 | tf_op jit(solution)/shard_map/ppermute | solution.py:180
  36.1 1.9 %collective-permute-start.5 = (bf16[1600,128]{1,0:T(8,128)(2,1)}, bf16[1600,128]{1,0:T(8,128)(2,1)S(1)}, u32[]{:S(2)}, u32[]{:S(2)}) collective-permute-start(bf16[1600,128]{1,0:T(8,128)(2,1)} %bitcast.3), channel_id=1, source_target_pairs={{0,2},{2,36},{4,6},{6,40},{8,10},{10,44},{12,14},{14,48},{16,18},{... | collective-permute-start | bytes 1228808 | tf_op jit(solution)/shard_map/ppermute | solution.py:180
  38.0 8.9 %all-to-all-done.bd_ref = bf16[8,104,1024]{2,1,0:T(8,128)(2,1)S(1)} async-done(((bf16[8,104,1024]{2,1,0:T(8,128)(2,1)}), bf16[8,104,1024]{2,1,0:T(8,128)(2,1)S(1)}, u32[]{:S(2)}, u32[]{:S(2)}) %all-to-all-start) | async-done | bytes 1703968 | tf_op jit(solution)/shard_map/all_to_all | solution.py:174
  46.9 0.1 reshape_squeeze.3.amp_ref
  47.0 0.0 collective-permute-done.2.ac00_ref
  47.0 0.0 collective-permute-done.3.ac01_ref
  47.0 1.8 %collective-permute-done.4.ac10_ref = bf16[1600,128]{1,0:T(8,128)(2,1)S(1)} collective-permute-done((bf16[1600,128]{1,0:T(8,128)(2,1)}, bf16[1600,128]{1,0:T(8,128)(2,1)S(1)}, u32[]{:S(2)}, u32[]{:S(2)}) %collective-permute-start.4) | collective-permute-done | bytes 409632 | tf_op jit(solution)/shard_map/ppermute | solution.py:180
  48.8 0.8 collective-permute-done.5.ac11_ref
  49.5 3.1 %multiply.3 = f32[8,160,128]{2,1,0:T(8,128)S(1)} custom-call(s32[1]{0:T(128)S(6)} %xor.3.m_ref, bf16[16,32]{1,0:T(8,128)(2,1)S(1)} %reshape_squeeze.3.amp_ref, bf16[1600,128]{1,0:T(8,128)(2,1)S(1)} %collective-permute-done.2.ac00_ref, bf16[1600,128]{1,0:T(8,128)(2,1)S(1)} %collective-permute-done.3.ac01_ref, ...), custom_call_target="tpu_custom_call" | custom-call | flops 1310720000 | bytes 6291456 | tf_op jit(solution)/shard_map/multiply/pallas_call | solution.py:122
  52.6 1.9 %collective-permute-start.6 = (f32[8,160,128]{2,1,0:T(8,128)S(1)}, f32[8,160,128]{2,1,0:T(8,128)S(1)}, u32[]{:S(2)}, u32[]{:S(2)}) collective-permute-start(f32[8,160,128]{2,1,0:T(8,128)S(1)} %multiply.3), channel_id=1, source_target_pairs={{0,32},{32,0},{1,33},{33,1},{2,34},{34,2},{3,35},{35,3},{4,36},{36... | collective-permute-start | bytes 1966088 | tf_op jit(solution)/shard_map/ppermute | solution.py:187
  54.6 3.1 %multiply.2 = f32[8,160,128]{2,1,0:T(8,128)S(1)} custom-call(s32[1]{0:T(128)} %bitcast.m_ref, bf16[16,32]{1,0:T(8,128)(2,1)S(1)} %reshape_squeeze.3.amp_ref, bf16[1600,128]{1,0:T(8,128)(2,1)S(1)} %collective-permute-done.2.ac00_ref, bf16[1600,128]{1,0:T(8,128)(2,1)S(1)} %collective-permute-done.3.ac01_ref, ...), custom_call_target="tpu_custom_call" | custom-call | flops 1310720000 | bytes 6291456 | tf_op jit(solution)/shard_map/multiply/pallas_call | solution.py:122
  57.7 0.0 collective-permute-done.6
  57.7 0.1 add_convert_fusion
  57.8 30.3 %all_to_all.10.parts_ref = bf16[8,160,128]{2,1,0:T(8,128)(2,1)S(1)} all-to-all(bf16[8,160,128]{2,1,0:T(8,128)(2,1)S(1)} %add_convert_fusion), channel_id=1, replica_groups={{16,17,24,25,0,1,8,9},{18,19,26,27,2,3,10,11},{20,21,28,29,4,5,12,13},{..., dimensions={0} | all-to-all | bytes 655360 | tf_op jit(solution)/shard_map/all_to_all | solution.py:189
  88.2 0.8 finish.1
  (1 shorter events, 0.0 us)
Async XLA Ops:
  0.0 11.7 %collective-permute-start = (bf16[100,8,128]{2,1,0:T(8,128)(2,1)}, bf16[100,8,128]{2,1,0:T(8,128)(2,1)S(1)}, u32[]{:S(2)}, u32[]{:S(2)}) collective-permute-start(bf16[100,8,128]{2,1,0:T(8,128)(2,1)} %param.4), channel_id=1, source_target_pairs={{0,64},{2,32},{4,0},{6,104},{8,72},{10,40},{12,8},{14,112},{16,80}... | collective-permute-start | bytes 614408 | tf_op jit(solution)/shard_map/ppermute | solution.py:171
  5.9 5.9 %collective-permute-start.1 = (bf16[4,8]{1,0:T(4,128)(2,1)}, bf16[4,8]{1,0:T(4,128)(2,1)S(1)}, u32[]{:S(2)}, u32[]{:S(2)}) collective-permute-start(bf16[4,8]{1,0:T(4,128)(2,1)} %bitcast.6), channel_id=1, source_target_pairs={{0,32},{32,0},{1,33},{33,1},{2,34},{34,2},{3,35},{35,3},{4,36},{36... | collective-permute-start | bytes 200 | tf_op jit(solution)/shard_map/ppermute | solution.py:173
  13.2 33.7 %all-to-all-start = ((bf16[8,104,1024]{2,1,0:T(8,128)(2,1)}), bf16[8,104,1024]{2,1,0:T(8,128)(2,1)S(1)}, u32[]{:S(2)}, u32[]{:S(2)}) async-start(bf16[8,104,1024]{2,1,0:T(8,128)(2,1)} %make_unit.1), calls=%async_computation | async-start | bytes 3407872 | tf_op jit(solution)/shard_map/all_to_all | solution.py:174
  24.0 23.0 %collective-permute-start.2 = (bf16[1600,128]{1,0:T(8,128)(2,1)}, bf16[1600,128]{1,0:T(8,128)(2,1)S(1)}, u32[]{:S(2)}, u32[]{:S(2)}) collective-permute-start(bf16[1600,128]{1,0:T(8,128)(2,1)} %bitcast.3), channel_id=1, source_target_pairs={{0,28},{2,38},{4,0},{6,42},{8,4},{10,46},{12,8},{14,50},{16,12},{1... | collective-permute-start | bytes 1228808 | tf_op jit(solution)/shard_map/ppermute | solution.py:180
  30.5 16.5 %collective-permute-start.3 = (bf16[1600,128]{1,0:T(8,128)(2,1)}, bf16[1600,128]{1,0:T(8,128)(2,1)S(1)}, u32[]{:S(2)}, u32[]{:S(2)}) collective-permute-start(bf16[1600,128]{1,0:T(8,128)(2,1)} %bitcast.3), channel_id=1, source_target_pairs={{0,30},{2,32},{4,2},{6,36},{8,6},{10,40},{12,10},{14,44},{16,14},{... | collective-permute-start | bytes 1228808 | tf_op jit(solution)/shard_map/ppermute | solution.py:180
  33.8 15.0 %collective-permute-start.4 = (bf16[1600,128]{1,0:T(8,128)(2,1)}, bf16[1600,128]{1,0:T(8,128)(2,1)S(1)}, u32[]{:S(2)}, u32[]{:S(2)}) collective-permute-start(bf16[1600,128]{1,0:T(8,128)(2,1)} %bitcast.3), channel_id=1, source_target_pairs={{0,0},{2,34},{4,4},{6,38},{8,8},{10,42},{12,12},{14,46},{16,16},{1... | collective-permute-start | bytes 1228808 | tf_op jit(solution)/shard_map/ppermute | solution.py:180
  36.1 13.5 %collective-permute-start.5 = (bf16[1600,128]{1,0:T(8,128)(2,1)}, bf16[1600,128]{1,0:T(8,128)(2,1)S(1)}, u32[]{:S(2)}, u32[]{:S(2)}) collective-permute-start(bf16[1600,128]{1,0:T(8,128)(2,1)} %bitcast.3), channel_id=1, source_target_pairs={{0,2},{2,36},{4,6},{6,40},{8,10},{10,44},{12,14},{14,48},{16,18},{... | collective-permute-start | bytes 1228808 | tf_op jit(solution)/shard_map/ppermute | solution.py:180
  52.6 5.1 %collective-permute-start.6 = (f32[8,160,128]{2,1,0:T(8,128)S(1)}, f32[8,160,128]{2,1,0:T(8,128)S(1)}, u32[]{:S(2)}, u32[]{:S(2)}) collective-permute-start(f32[8,160,128]{2,1,0:T(8,128)S(1)} %multiply.3), channel_id=1, source_target_pairs={{0,32},{32,0},{1,33},{33,1},{2,34},{34,2},{3,35},{35,3},{4,36},{36... | collective-permute-start | bytes 1966088 | tf_op jit(solution)/shard_map/ppermute | solution.py:187

commit v7 on v6

--- a/solution.py
+++ b/solution.py
@@ -108,7 +108,7 @@
     )
     for t in range(8):
         at = slice(HALF * t, HALF * (t + 1))
-        to = 2 * ORDER.index(t // 2) + t % 2
+        to = 2 * ORDER.index(t // 2) + 1 - t % 2
         last = acc_ref[at, 3 * WIDE:3 * WIDE + NA]
         for j in range(3):
             out_ref[to, 50 * j:50 * j + 50, :] = jnp.concatenate(
@@ -157,7 +157,7 @@
 
 
 def home(z, delta):
-    two = 2 if (z - delta) % 2 == 0 else -2
+    two = -2 if (z - delta) % 2 == 0 else 2
     return (z - (0, 1, two, -1)[delta]) % 16
 
 
@@ -185,7 +185,7 @@
     for_other = multiply(m ^ 1, amp, blocks, bd)
     for_self = multiply(m, amp, blocks, bd)
     pieces = (for_self + lax.ppermute(for_other, "core", [(0, 1), (1, 0)])).astype(jnp.bfloat16)
-    groups = [[8 * zq + 2 * f + y for zq in ORDER for y in range(2)] for f in range(4)]
+    groups = [[8 * zq + 2 * f + y for zq in ORDER for y in (1, 0)] for f in range(4)]
     summed = finish(lax.all_to_all(pieces, COL, 0, 0, axis_index_groups=groups, tiled=True))
     return jnp.transpose(summed, (1, 2, 0))
 

time: 89.4 us -> 87.1 us (0.974)
  blocking collectives: 30.3 us -> 28 us
    all_to_all x1, blocking collectives: 30.3 us -> 28 us  [on_device(): lax.all_to_all(pieces, COL, 0, 0, axis_index_groups=groups, tiled=True)]
    ppermute x4, waiting for transfers between devices: 2.53 us -> 1.33 us  [on_device(): blocks[h, m] = lax.ppermute(ac, ('core', 'zq', 'zl'), ways)]
  transfers between devices with their start and end apart: 8 -> 8, of which waited for: 4 -> 3; matrix products, arithmetic and copies ran while one was open for 1% -> 1% of each run, Pallas kernels for 4% -> 4%
where the time goes in v7:
time: 87.1 us; the launch traced here: 86.3 us
  starting transfers between devices  37.8 us (43%)
  blocking collectives  28 us (32%)
  waiting for transfers between devices  10.9 us (13%)
  Pallas kernels  8.58 us (10%)
    all_to_all x1, blocking collectives, on_device(): lax.all_to_all(pieces, COL, 0, 0, axis_index_groups=groups, tiled=True)  28 us
    ppermute x4, starting transfers between devices, on_device(): blocks[h, m] = lax.ppermute(ac, ('core', 'zq', 'zl'), ways)  13.5 us
    all_to_all x1, starting transfers between devices, on_device(): lax.all_to_all(make_unit(core.astype(jnp.int32)[None], shard, amp.astype(...  11.7 us
    all_to_all x1, waiting for transfers between devices, on_device(): lax.all_to_all(make_unit(core.astype(jnp.int32)[None], shard, amp.astype(...  9.28 us
    pallas_call x2, Pallas kernels, multiply(): pl.pallas_call(product_kernel, in_specs=[pl.BlockSpec(memory_space=pltpu....  6.25 us
    ppermute x1, starting transfers between devices, on_device(): shard = lax.ppermute(fitted_bd, ('xl', 'core', 'zq', 'zl'), ways)  5.85 us
    ppermute x1, starting transfers between devices, on_device(): peer = lax.ppermute(amp, 'core', [(0, 1), (1, 0)])  4.84 us
    ppermute x1, starting transfers between devices, on_device(): lax.ppermute(for_other, 'core', [(0, 1), (1, 0)])  1.92 us
  transfers between devices with their start and end apart: 8, of which 3 were waited for; matrix products, arithmetic and copies ran while one was open for 1% of the time, Pallas kernels for 4%

profile of v7, /device:TPU:1, one launch (start us, length us, event | category | flops | bytes accessed | tf_op | source)
XLA Modules:
  0.0 86.3 jit_solution(5000214233089928749)
XLA Ops:
  0.0 5.9 %collective-permute-start = (bf16[100,8,128]{2,1,0:T(8,128)(2,1)}, bf16[100,8,128]{2,1,0:T(8,128)(2,1)S(1)}, u32[]{:S(2)}, u32[]{:S(2)}) collective-permute-start(bf16[100,8,128]{2,1,0:T(8,128)(2,1)} %param.4), channel_id=1, source_target_pairs={{0,64},{2,32},{4,8},{6,104},{8,72},{10,40},{12,16},{14,112},{16,80... | collective-permute-start | bytes 614408 | tf_op jit(solution)/shard_map/ppermute | solution.py:171
  5.9 4.8 %collective-permute-start.1 = (bf16[4,8]{1,0:T(4,128)(2,1)}, bf16[4,8]{1,0:T(4,128)(2,1)S(1)}, u32[]{:S(2)}, u32[]{:S(2)}) collective-permute-start(bf16[4,8]{1,0:T(4,128)(2,1)} %bitcast.6), channel_id=1, source_target_pairs={{0,32},{32,0},{1,33},{33,1},{2,34},{34,2},{3,35},{35,3},{4,36},{36... | collective-permute-start | bytes 200 | tf_op jit(solution)/shard_map/ppermute | solution.py:173
  10.7 0.7 bitcast_convert_fusion.amp_ref
  11.4 0.3 collective-permute-done.1.peer_ref
  11.7 0.0 collective-permute-done.bd_ref
  11.7 1.5 %make_unit.1 = bf16[8,104,1024]{2,1,0:T(8,128)(2,1)} custom-call(s32[1]{0:T(128)} %bitcast.1.core_ref, bf16[100,8,128]{2,1,0:T(8,128)(2,1)S(1)} %collective-permute-done.bd_ref, f32[4,8]{1,0:T(4,128)S(1)} %bitcast_convert_fusion.amp_ref, bf16[4,8]{1,0:T(4,128)(2,1)S(1)} %collective-permute-done.1.peer_ref), custom_call_target="tpu_custom_call" | custom-call | tf_op jit(solution)/shard_map/make_unit/pallas_call | solution.py:67
  13.2 11.7 %all-to-all-start = ((bf16[8,104,1024]{2,1,0:T(8,128)(2,1)}), bf16[8,104,1024]{2,1,0:T(8,128)(2,1)S(1)}, u32[]{:S(2)}, u32[]{:S(2)}) async-start(bf16[8,104,1024]{2,1,0:T(8,128)(2,1)} %make_unit.1), calls=%async_computation | async-start | bytes 3407872 | tf_op jit(solution)/shard_map/all_to_all | solution.py:174
  24.9 6.0 %collective-permute-start.2 = (bf16[1600,128]{1,0:T(8,128)(2,1)}, bf16[1600,128]{1,0:T(8,128)(2,1)S(1)}, u32[]{:S(2)}, u32[]{:S(2)}) collective-permute-start(bf16[1600,128]{1,0:T(8,128)(2,1)} %bitcast.3), channel_id=1, source_target_pairs={{0,4},{2,62},{4,8},{6,34},{8,12},{10,38},{12,16},{14,42},{16,20},{... | collective-permute-start | bytes 1228808 | tf_op jit(solution)/shard_map/ppermute | solution.py:180
  30.9 1.9 %collective-permute-start.3 = (bf16[1600,128]{1,0:T(8,128)(2,1)}, bf16[1600,128]{1,0:T(8,128)(2,1)S(1)}, u32[]{:S(2)}, u32[]{:S(2)}) collective-permute-start(bf16[1600,128]{1,0:T(8,128)(2,1)} %bitcast.3), channel_id=1, source_target_pairs={{0,30},{2,32},{4,2},{6,36},{8,6},{10,40},{12,10},{14,44},{16,14},{... | collective-permute-start | bytes 1228808 | tf_op jit(solution)/shard_map/ppermute | solution.py:180
  32.9 3.6 %collective-permute-start.4 = (bf16[1600,128]{1,0:T(8,128)(2,1)}, bf16[1600,128]{1,0:T(8,128)(2,1)S(1)}, u32[]{:S(2)}, u32[]{:S(2)}) collective-permute-start(bf16[1600,128]{1,0:T(8,128)(2,1)} %bitcast.3), channel_id=1, source_target_pairs={{0,0},{2,34},{4,4},{6,38},{8,8},{10,42},{12,12},{14,46},{16,16},{1... | collective-permute-start | bytes 1228808 | tf_op jit(solution)/shard_map/ppermute | solution.py:180
  36.5 1.9 %collective-permute-start.5 = (bf16[1600,128]{1,0:T(8,128)(2,1)}, bf16[1600,128]{1,0:T(8,128)(2,1)S(1)}, u32[]{:S(2)}, u32[]{:S(2)}) collective-permute-start(bf16[1600,128]{1,0:T(8,128)(2,1)} %bitcast.3), channel_id=1, source_target_pairs={{0,2},{2,36},{4,6},{6,40},{8,10},{10,44},{12,14},{14,48},{16,18},{... | collective-permute-start | bytes 1228808 | tf_op jit(solution)/shard_map/ppermute | solution.py:180
  38.4 9.3 %all-to-all-done.bd_ref = bf16[8,104,1024]{2,1,0:T(8,128)(2,1)S(1)} async-done(((bf16[8,104,1024]{2,1,0:T(8,128)(2,1)}), bf16[8,104,1024]{2,1,0:T(8,128)(2,1)S(1)}, u32[]{:S(2)}, u32[]{:S(2)}) %all-to-all-start) | async-done | bytes 1703968 | tf_op jit(solution)/shard_map/all_to_all | solution.py:174
  47.8 0.1 reshape_squeeze.3.amp_ref
  47.8 0.0 collective-permute-done.2.ac00_ref
  47.8 0.0 collective-permute-done.3.ac01_ref
  47.8 0.0 collective-permute-done.4.ac10_ref
  47.8 1.3 %collective-permute-done.5.ac11_ref = bf16[1600,128]{1,0:T(8,128)(2,1)S(1)} collective-permute-done((bf16[1600,128]{1,0:T(8,128)(2,1)}, bf16[1600,128]{1,0:T(8,128)(2,1)S(1)}, u32[]{:S(2)}, u32[]{:S(2)}) %collective-permute-start.5) | collective-permute-done | bytes 409632 | tf_op jit(solution)/shard_map/ppermute | solution.py:180
  49.2 3.1 %multiply.3 = f32[8,160,128]{2,1,0:T(8,128)S(1)} custom-call(s32[1]{0:T(128)S(6)} %xor.3.m_ref, bf16[16,32]{1,0:T(8,128)(2,1)S(1)} %reshape_squeeze.3.amp_ref, bf16[1600,128]{1,0:T(8,128)(2,1)S(1)} %collective-permute-done.2.ac00_ref, bf16[1600,128]{1,0:T(8,128)(2,1)S(1)} %collective-permute-done.3.ac01_ref, ...), custom_call_target="tpu_custom_call" | custom-call | flops 1310720000 | bytes 6291456 | tf_op jit(solution)/shard_map/multiply/pallas_call | solution.py:122
  52.3 1.9 %collective-permute-start.6 = (f32[8,160,128]{2,1,0:T(8,128)S(1)}, f32[8,160,128]{2,1,0:T(8,128)S(1)}, u32[]{:S(2)}, u32[]{:S(2)}) collective-permute-start(f32[8,160,128]{2,1,0:T(8,128)S(1)} %multiply.3), channel_id=1, source_target_pairs={{0,32},{32,0},{1,33},{33,1},{2,34},{34,2},{3,35},{35,3},{4,36},{36... | collective-permute-start | bytes 1966088 | tf_op jit(solution)/shard_map/ppermute | solution.py:187
  54.2 3.1 %multiply.2 = f32[8,160,128]{2,1,0:T(8,128)S(1)} custom-call(s32[1]{0:T(128)} %bitcast.m_ref, bf16[16,32]{1,0:T(8,128)(2,1)S(1)} %reshape_squeeze.3.amp_ref, bf16[1600,128]{1,0:T(8,128)(2,1)S(1)} %collective-permute-done.2.ac00_ref, bf16[1600,128]{1,0:T(8,128)(2,1)S(1)} %collective-permute-done.3.ac01_ref, ...), custom_call_target="tpu_custom_call" | custom-call | flops 1310720000 | bytes 6291456 | tf_op jit(solution)/shard_map/multiply/pallas_call | solution.py:122
  57.4 0.0 collective-permute-done.6
  57.4 0.1 add_convert_fusion
  57.5 28.0 %all_to_all.10.parts_ref = bf16[8,160,128]{2,1,0:T(8,128)(2,1)S(1)} all-to-all(bf16[8,160,128]{2,1,0:T(8,128)(2,1)S(1)} %add_convert_fusion), channel_id=1, replica_groups={{17,16,25,24,1,0,9,8},{19,18,27,26,3,2,11,10},{21,20,29,28,5,4,13,12},{..., dimensions={0} | all-to-all | bytes 655360 | tf_op jit(solution)/shard_map/all_to_all | solution.py:189
  85.5 0.8 finish.1
  (1 shorter events, 0.0 us)
Async XLA Ops:
  0.0 11.7 %collective-permute-start = (bf16[100,8,128]{2,1,0:T(8,128)(2,1)}, bf16[100,8,128]{2,1,0:T(8,128)(2,1)S(1)}, u32[]{:S(2)}, u32[]{:S(2)}) collective-permute-start(bf16[100,8,128]{2,1,0:T(8,128)(2,1)} %param.4), channel_id=1, source_target_pairs={{0,64},{2,32},{4,8},{6,104},{8,72},{10,40},{12,16},{14,112},{16,80... | collective-permute-start | bytes 614408 | tf_op jit(solution)/shard_map/ppermute | solution.py:171
  5.9 5.9 %collective-permute-start.1 = (bf16[4,8]{1,0:T(4,128)(2,1)}, bf16[4,8]{1,0:T(4,128)(2,1)S(1)}, u32[]{:S(2)}, u32[]{:S(2)}) collective-permute-start(bf16[4,8]{1,0:T(4,128)(2,1)} %bitcast.6), channel_id=1, source_target_pairs={{0,32},{32,0},{1,33},{33,1},{2,34},{34,2},{3,35},{35,3},{4,36},{36... | collective-permute-start | bytes 200 | tf_op jit(solution)/shard_map/ppermute | solution.py:173
  13.2 34.5 %all-to-all-start = ((bf16[8,104,1024]{2,1,0:T(8,128)(2,1)}), bf16[8,104,1024]{2,1,0:T(8,128)(2,1)S(1)}, u32[]{:S(2)}, u32[]{:S(2)}) async-start(bf16[8,104,1024]{2,1,0:T(8,128)(2,1)} %make_unit.1), calls=%async_computation | async-start | bytes 3407872 | tf_op jit(solution)/shard_map/all_to_all | solution.py:174
  24.9 22.9 %collective-permute-start.2 = (bf16[1600,128]{1,0:T(8,128)(2,1)}, bf16[1600,128]{1,0:T(8,128)(2,1)S(1)}, u32[]{:S(2)}, u32[]{:S(2)}) collective-permute-start(bf16[1600,128]{1,0:T(8,128)(2,1)} %bitcast.3), channel_id=1, source_target_pairs={{0,4},{2,62},{4,8},{6,34},{8,12},{10,38},{12,16},{14,42},{16,20},{... | collective-permute-start | bytes 1228808 | tf_op jit(solution)/shard_map/ppermute | solution.py:180
  30.9 16.9 %collective-permute-start.3 = (bf16[1600,128]{1,0:T(8,128)(2,1)}, bf16[1600,128]{1,0:T(8,128)(2,1)S(1)}, u32[]{:S(2)}, u32[]{:S(2)}) collective-permute-start(bf16[1600,128]{1,0:T(8,128)(2,1)} %bitcast.3), channel_id=1, source_target_pairs={{0,30},{2,32},{4,2},{6,36},{8,6},{10,40},{12,10},{14,44},{16,14},{... | collective-permute-start | bytes 1228808 | tf_op jit(solution)/shard_map/ppermute | solution.py:180
  32.9 15.0 %collective-permute-start.4 = (bf16[1600,128]{1,0:T(8,128)(2,1)}, bf16[1600,128]{1,0:T(8,128)(2,1)S(1)}, u32[]{:S(2)}, u32[]{:S(2)}) collective-permute-start(bf16[1600,128]{1,0:T(8,128)(2,1)} %bitcast.3), channel_id=1, source_target_pairs={{0,0},{2,34},{4,4},{6,38},{8,8},{10,42},{12,12},{14,46},{16,16},{1... | collective-permute-start | bytes 1228808 | tf_op jit(solution)/shard_map/ppermute | solution.py:180
  36.5 12.7 %collective-permute-start.5 = (bf16[1600,128]{1,0:T(8,128)(2,1)}, bf16[1600,128]{1,0:T(8,128)(2,1)S(1)}, u32[]{:S(2)}, u32[]{:S(2)}) collective-permute-start(bf16[1600,128]{1,0:T(8,128)(2,1)} %bitcast.3), channel_id=1, source_target_pairs={{0,2},{2,36},{4,6},{6,40},{8,10},{10,44},{12,14},{14,48},{16,18},{... | collective-permute-start | bytes 1228808 | tf_op jit(solution)/shard_map/ppermute | solution.py:180
  52.3 5.1 %collective-permute-start.6 = (f32[8,160,128]{2,1,0:T(8,128)S(1)}, f32[8,160,128]{2,1,0:T(8,128)S(1)}, u32[]{:S(2)}, u32[]{:S(2)}) collective-permute-start(f32[8,160,128]{2,1,0:T(8,128)S(1)} %multiply.3), channel_id=1, source_target_pairs={{0,32},{32,0},{1,33},{33,1},{2,34},{34,2},{3,35},{35,3},{4,36},{36... | collective-permute-start | bytes 1966088 | tf_op jit(solution)/shard_map/ppermute | solution.py:187

commit v8 on v7

--- a/solution.py
+++ b/solution.py
@@ -7,6 +7,7 @@
 
 ROW = ("yl", "xh", "xl", "core")
 COL = ("zq", "zl", "yh")
+FLIP = 6
 ORDER = (2, 3, 0, 1)
 DELTA = ((2, 1), (0, 3))
 HALF_OF = (1, 0, 0, 1)
@@ -28,7 +29,7 @@
     pick_row = jnp.where(row // wide == col, 1.0, 0.0).astype(jnp.bfloat16)
     row = lax.broadcasted_iota(jnp.int32, (C, across), 0)
     col = lax.broadcasted_iota(jnp.int32, (C, across), 1)
-    pick_col = jnp.where(col % C == row, 1.0, 0.0).astype(jnp.bfloat16)
+    pick_col = jnp.where(col % C == row ^ (2 * FLIP), 1.0, 0.0).astype(jnp.bfloat16)
     wider = jnp.dot(pick_row, amp.T, preferred_element_type=jnp.float32).astype(jnp.bfloat16)
     full = jnp.dot(wider, pick_col, preferred_element_type=jnp.float32)
     row = lax.broadcasted_iota(jnp.int32, (tall, across), 0)
@@ -89,7 +90,7 @@
 
     for h in range(2):
         for t in range(4):
-            left_ref[NB * t:NB * (t + 1), h * D * Q:(h + 1) * D * Q] = bd_ref[2 * t + h, 0:NB, :]
+            left_ref[NB * t:NB * (t + 1), h * D * Q:(h + 1) * D * Q] = bd_ref[(2 * t + h) ^ FLIP, 0:NB, :]
     w16, w4 = spread(amp_ref[...], 16), spread(amp_ref[...], 4)
     for k in range(7):
         w, n = (w16, 16) if k < 6 else (w4, 4)
@@ -171,7 +172,7 @@
     shard = lax.ppermute(fitted_bd, ("xl", "core", "zq", "zl"), ways)
     amp = amplitudes.reshape(NP, D)
     peer = lax.ppermute(amp, "core", [(0, 1), (1, 0)])
-    bd = lax.all_to_all(make_unit(core.astype(jnp.int32)[None], shard, amp.astype(jnp.float32), peer), ("yl", "xh", "xl"), 0, 0, tiled=True)
+    bd = lax.all_to_all(make_unit(core.astype(jnp.int32)[None], shard, amp.astype(jnp.float32), peer), ("yl", "xh", "xl"), 0, 0, axis_index_groups=[[i ^ FLIP for i in range(8)]], tiled=True)
     ac = fitted_ac.reshape(NA * C, Q)
     blocks = {}
     for h in range(2):

time: 87.1 us -> 88.9 us (1.021)
  starting transfers between devices: 37.8 us -> 40 us
    all_to_all x1, starting transfers between devices: 11.7 us -> 12.9 us  [on_device(): lax.all_to_all(make_unit(core.astype(jnp.int32)[None], shard, amp.astype(...]
    ppermute x4, starting transfers between devices: 13.5 us -> 14.6 us  [on_device(): blocks[h, m] = lax.ppermute(ac, ('core', 'zq', 'zl'), ways)]
where the time goes in v8:
time: 88.9 us; the launch traced here: 88.5 us
  starting transfers between devices  40 us (45%)
  blocking collectives  28 us (31%)
  waiting for transfers between devices  10.9 us (12%)
  Pallas kernels  8.58 us (10%)
    all_to_all x1, blocking collectives, on_device(): lax.all_to_all(pieces, COL, 0, 0, axis_index_groups=groups, tiled=True)  28 us
    ppermute x4, starting transfers between devices, on_device(): blocks[h, m] = lax.ppermute(ac, ('core', 'zq', 'zl'), ways)  14.6 us
    all_to_all x1, starting transfers between devices, on_device(): lax.all_to_all(make_unit(core.astype(jnp.int32)[None], shard, amp.astype(...  12.9 us
    all_to_all x1, waiting for transfers between devices, on_device(): lax.all_to_all(make_unit(core.astype(jnp.int32)[None], shard, amp.astype(...  9.09 us
    pallas_call x2, Pallas kernels, multiply(): pl.pallas_call(product_kernel, in_specs=[pl.BlockSpec(memory_space=pltpu....  6.25 us
    ppermute x1, starting transfers between devices, on_device(): shard = lax.ppermute(fitted_bd, ('xl', 'core', 'zq', 'zl'), ways)  5.85 us
    ppermute x1, starting transfers between devices, on_device(): peer = lax.ppermute(amp, 'core', [(0, 1), (1, 0)])  4.84 us
    ppermute x1, starting transfers between devices, on_device(): lax.ppermute(for_other, 'core', [(0, 1), (1, 0)])  1.92 us
  transfers between devices with their start and end apart: 8, of which 3 were waited for; matrix products, arithmetic and copies ran while one was open for 1% of the time, Pallas kernels for 4%

profile of v8, /device:TPU:1, one launch (start us, length us, event | category | flops | bytes accessed | tf_op | source)
XLA Modules:
  0.0 88.5 jit_solution(7453845491932057111)
XLA Ops:
  0.0 5.9 %collective-permute-start = (bf16[100,8,128]{2,1,0:T(8,128)(2,1)}, bf16[100,8,128]{2,1,0:T(8,128)(2,1)S(1)}, u32[]{:S(2)}, u32[]{:S(2)}) collective-permute-start(bf16[100,8,128]{2,1,0:T(8,128)(2,1)} %param.4), channel_id=1, source_target_pairs={{0,64},{2,32},{4,8},{6,104},{8,72},{10,40},{12,16},{14,112},{16,80... | collective-permute-start | bytes 614408 | tf_op jit(solution)/shard_map/ppermute | solution.py:172
  5.9 4.8 %collective-permute-start.1 = (bf16[4,8]{1,0:T(4,128)(2,1)}, bf16[4,8]{1,0:T(4,128)(2,1)S(1)}, u32[]{:S(2)}, u32[]{:S(2)}) collective-permute-start(bf16[4,8]{1,0:T(4,128)(2,1)} %bitcast.6), channel_id=1, source_target_pairs={{0,32},{32,0},{1,33},{33,1},{2,34},{34,2},{3,35},{35,3},{4,36},{36... | collective-permute-start | bytes 200 | tf_op jit(solution)/shard_map/ppermute | solution.py:174
  10.7 0.7 bitcast_convert_fusion.amp_ref
  11.4 0.3 collective-permute-done.1.peer_ref
  11.7 0.0 collective-permute-done.bd_ref
  11.7 1.5 %make_unit.1 = bf16[8,104,1024]{2,1,0:T(8,128)(2,1)} custom-call(s32[1]{0:T(128)} %bitcast.1.core_ref, bf16[100,8,128]{2,1,0:T(8,128)(2,1)S(1)} %collective-permute-done.bd_ref, f32[4,8]{1,0:T(4,128)S(1)} %bitcast_convert_fusion.amp_ref, bf16[4,8]{1,0:T(4,128)(2,1)S(1)} %collective-permute-done.1.peer_ref), custom_call_target="tpu_custom_call" | custom-call | tf_op jit(solution)/shard_map/make_unit/pallas_call | solution.py:68
  13.2 12.9 %all-to-all-start = ((bf16[8,104,1024]{2,1,0:T(8,128)(2,1)}), bf16[8,104,1024]{2,1,0:T(8,128)(2,1)S(1)}, u32[]{:S(2)}, u32[]{:S(2)}) async-start(bf16[8,104,1024]{2,1,0:T(8,128)(2,1)} %make_unit.1), calls=%async_computation | async-start | bytes 3407872 | tf_op jit(solution)/shard_map/all_to_all | solution.py:175
  26.1 7.1 %collective-permute-start.2 = (bf16[1600,128]{1,0:T(8,128)(2,1)}, bf16[1600,128]{1,0:T(8,128)(2,1)S(1)}, u32[]{:S(2)}, u32[]{:S(2)}) collective-permute-start(bf16[1600,128]{1,0:T(8,128)(2,1)} %bitcast.3), channel_id=1, source_target_pairs={{0,4},{2,62},{4,8},{6,34},{8,12},{10,38},{12,16},{14,42},{16,20},{... | collective-permute-start | bytes 1228808 | tf_op jit(solution)/shard_map/ppermute | solution.py:181
  33.2 1.9 %collective-permute-start.3 = (bf16[1600,128]{1,0:T(8,128)(2,1)}, bf16[1600,128]{1,0:T(8,128)(2,1)S(1)}, u32[]{:S(2)}, u32[]{:S(2)}) collective-permute-start(bf16[1600,128]{1,0:T(8,128)(2,1)} %bitcast.3), channel_id=1, source_target_pairs={{0,30},{2,32},{4,2},{6,36},{8,6},{10,40},{12,10},{14,44},{16,14},{... | collective-permute-start | bytes 1228808 | tf_op jit(solution)/shard_map/ppermute | solution.py:181
  35.1 3.6 %collective-permute-start.4 = (bf16[1600,128]{1,0:T(8,128)(2,1)}, bf16[1600,128]{1,0:T(8,128)(2,1)S(1)}, u32[]{:S(2)}, u32[]{:S(2)}) collective-permute-start(bf16[1600,128]{1,0:T(8,128)(2,1)} %bitcast.3), channel_id=1, source_target_pairs={{0,0},{2,34},{4,4},{6,38},{8,8},{10,42},{12,12},{14,46},{16,16},{1... | collective-permute-start | bytes 1228808 | tf_op jit(solution)/shard_map/ppermute | solution.py:181
  38.7 1.9 %collective-permute-start.5 = (bf16[1600,128]{1,0:T(8,128)(2,1)}, bf16[1600,128]{1,0:T(8,128)(2,1)S(1)}, u32[]{:S(2)}, u32[]{:S(2)}) collective-permute-start(bf16[1600,128]{1,0:T(8,128)(2,1)} %bitcast.3), channel_id=1, source_target_pairs={{0,2},{2,36},{4,6},{6,40},{8,10},{10,44},{12,14},{14,48},{16,18},{... | collective-permute-start | bytes 1228808 | tf_op jit(solution)/shard_map/ppermute | solution.py:181
  40.7 9.1 %all-to-all-done.bd_ref = bf16[8,104,1024]{2,1,0:T(8,128)(2,1)S(1)} async-done(((bf16[8,104,1024]{2,1,0:T(8,128)(2,1)}), bf16[8,104,1024]{2,1,0:T(8,128)(2,1)S(1)}, u32[]{:S(2)}, u32[]{:S(2)}) %all-to-all-start) | async-done | bytes 1703968 | tf_op jit(solution)/shard_map/all_to_all | solution.py:175
  49.8 0.1 reshape_squeeze.3.amp_ref
  49.9 0.0 collective-permute-done.2.ac00_ref
  49.9 0.0 collective-permute-done.3.ac01_ref
  49.9 0.0 collective-permute-done.4.ac10_ref
  49.9 1.5 %collective-permute-done.5.ac11_ref = bf16[1600,128]{1,0:T(8,128)(2,1)S(1)} collective-permute-done((bf16[1600,128]{1,0:T(8,128)(2,1)}, bf16[1600,128]{1,0:T(8,128)(2,1)S(1)}, u32[]{:S(2)}, u32[]{:S(2)}) %collective-permute-start.5) | collective-permute-done | bytes 409632 | tf_op jit(solution)/shard_map/ppermute | solution.py:181
  51.4 3.1 %multiply.3 = f32[8,160,128]{2,1,0:T(8,128)S(1)} custom-call(s32[1]{0:T(128)S(6)} %xor.3.m_ref, bf16[16,32]{1,0:T(8,128)(2,1)S(1)} %reshape_squeeze.3.amp_ref, bf16[1600,128]{1,0:T(8,128)(2,1)S(1)} %collective-permute-done.2.ac00_ref, bf16[1600,128]{1,0:T(8,128)(2,1)S(1)} %collective-permute-done.3.ac01_ref, ...), custom_call_target="tpu_custom_call" | custom-call | flops 1310720000 | bytes 6291456 | tf_op jit(solution)/shard_map/multiply/pallas_call | solution.py:123
  54.5 1.9 %collective-permute-start.6 = (f32[8,160,128]{2,1,0:T(8,128)S(1)}, f32[8,160,128]{2,1,0:T(8,128)S(1)}, u32[]{:S(2)}, u32[]{:S(2)}) collective-permute-start(f32[8,160,128]{2,1,0:T(8,128)S(1)} %multiply.3), channel_id=1, source_target_pairs={{0,32},{32,0},{1,33},{33,1},{2,34},{34,2},{3,35},{35,3},{4,36},{36... | collective-permute-start | bytes 1966088 | tf_op jit(solution)/shard_map/ppermute | solution.py:188
  56.5 3.1 %multiply.2 = f32[8,160,128]{2,1,0:T(8,128)S(1)} custom-call(s32[1]{0:T(128)} %bitcast.m_ref, bf16[16,32]{1,0:T(8,128)(2,1)S(1)} %reshape_squeeze.3.amp_ref, bf16[1600,128]{1,0:T(8,128)(2,1)S(1)} %collective-permute-done.2.ac00_ref, bf16[1600,128]{1,0:T(8,128)(2,1)S(1)} %collective-permute-done.3.ac01_ref, ...), custom_call_target="tpu_custom_call" | custom-call | flops 1310720000 | bytes 6291456 | tf_op jit(solution)/shard_map/multiply/pallas_call | solution.py:123
  59.6 0.0 collective-permute-done.6
  59.6 0.1 add_convert_fusion
  59.7 28.0 %all_to_all.10.parts_ref = bf16[8,160,128]{2,1,0:T(8,128)(2,1)S(1)} all-to-all(bf16[8,160,128]{2,1,0:T(8,128)(2,1)S(1)} %add_convert_fusion), channel_id=1, replica_groups={{17,16,25,24,1,0,9,8},{19,18,27,26,3,2,11,10},{21,20,29,28,5,4,13,12},{..., dimensions={0} | all-to-all | bytes 655360 | tf_op jit(solution)/shard_map/all_to_all | solution.py:190
  87.7 0.8 finish.1
  (1 shorter events, 0.0 us)
Async XLA Ops:
  0.0 11.7 %collective-permute-start = (bf16[100,8,128]{2,1,0:T(8,128)(2,1)}, bf16[100,8,128]{2,1,0:T(8,128)(2,1)S(1)}, u32[]{:S(2)}, u32[]{:S(2)}) collective-permute-start(bf16[100,8,128]{2,1,0:T(8,128)(2,1)} %param.4), channel_id=1, source_target_pairs={{0,64},{2,32},{4,8},{6,104},{8,72},{10,40},{12,16},{14,112},{16,80... | collective-permute-start | bytes 614408 | tf_op jit(solution)/shard_map/ppermute | solution.py:172
  5.9 5.9 %collective-permute-start.1 = (bf16[4,8]{1,0:T(4,128)(2,1)}, bf16[4,8]{1,0:T(4,128)(2,1)S(1)}, u32[]{:S(2)}, u32[]{:S(2)}) collective-permute-start(bf16[4,8]{1,0:T(4,128)(2,1)} %bitcast.6), channel_id=1, source_target_pairs={{0,32},{32,0},{1,33},{33,1},{2,34},{34,2},{3,35},{35,3},{4,36},{36... | collective-permute-start | bytes 200 | tf_op jit(solution)/shard_map/ppermute | solution.py:174
  13.2 36.5 %all-to-all-start = ((bf16[8,104,1024]{2,1,0:T(8,128)(2,1)}), bf16[8,104,1024]{2,1,0:T(8,128)(2,1)S(1)}, u32[]{:S(2)}, u32[]{:S(2)}) async-start(bf16[8,104,1024]{2,1,0:T(8,128)(2,1)} %make_unit.1), calls=%async_computation | async-start | bytes 3407872 | tf_op jit(solution)/shard_map/all_to_all | solution.py:175
  26.1 23.8 %collective-permute-start.2 = (bf16[1600,128]{1,0:T(8,128)(2,1)}, bf16[1600,128]{1,0:T(8,128)(2,1)S(1)}, u32[]{:S(2)}, u32[]{:S(2)}) collective-permute-start(bf16[1600,128]{1,0:T(8,128)(2,1)} %bitcast.3), channel_id=1, source_target_pairs={{0,4},{2,62},{4,8},{6,34},{8,12},{10,38},{12,16},{14,42},{16,20},{... | collective-permute-start | bytes 1228808 | tf_op jit(solution)/shard_map/ppermute | solution.py:181
  33.2 16.7 %collective-permute-start.3 = (bf16[1600,128]{1,0:T(8,128)(2,1)}, bf16[1600,128]{1,0:T(8,128)(2,1)S(1)}, u32[]{:S(2)}, u32[]{:S(2)}) collective-permute-start(bf16[1600,128]{1,0:T(8,128)(2,1)} %bitcast.3), channel_id=1, source_target_pairs={{0,30},{2,32},{4,2},{6,36},{8,6},{10,40},{12,10},{14,44},{16,14},{... | collective-permute-start | bytes 1228808 | tf_op jit(solution)/shard_map/ppermute | solution.py:181
  35.1 14.8 %collective-permute-start.4 = (bf16[1600,128]{1,0:T(8,128)(2,1)}, bf16[1600,128]{1,0:T(8,128)(2,1)S(1)}, u32[]{:S(2)}, u32[]{:S(2)}) collective-permute-start(bf16[1600,128]{1,0:T(8,128)(2,1)} %bitcast.3), channel_id=1, source_target_pairs={{0,0},{2,34},{4,4},{6,38},{8,8},{10,42},{12,12},{14,46},{16,16},{1... | collective-permute-start | bytes 1228808 | tf_op jit(solution)/shard_map/ppermute | solution.py:181
  38.7 12.7 %collective-permute-start.5 = (bf16[1600,128]{1,0:T(8,128)(2,1)}, bf16[1600,128]{1,0:T(8,128)(2,1)S(1)}, u32[]{:S(2)}, u32[]{:S(2)}) collective-permute-start(bf16[1600,128]{1,0:T(8,128)(2,1)} %bitcast.3), channel_id=1, source_target_pairs={{0,2},{2,36},{4,6},{6,40},{8,10},{10,44},{12,14},{14,48},{16,18},{... | collective-permute-start | bytes 1228808 | tf_op jit(solution)/shard_map/ppermute | solution.py:181
  54.5 5.1 %collective-permute-start.6 = (f32[8,160,128]{2,1,0:T(8,128)S(1)}, f32[8,160,128]{2,1,0:T(8,128)S(1)}, u32[]{:S(2)}, u32[]{:S(2)}) collective-permute-start(f32[8,160,128]{2,1,0:T(8,128)S(1)} %multiply.3), channel_id=1, source_target_pairs={{0,32},{32,0},{1,33},{33,1},{2,34},{34,2},{3,35},{35,3},{4,36},{36... | collective-permute-start | bytes 1966088 | tf_op jit(solution)/shard_map/ppermute | solution.py:188
